TPU v7x, 32 devices: a whole 2x2x4 slice. The times are simulated.
32 devices in a mesh: tile: 8 (over z, x), lev: 4 (over y, core).
Axes of the slice: x: 2, y: 2, z: 4, core: 2. Of those that a mesh axis runs over, the one named last changes fastest.
Arguments:
- control_static: float32 [2, 128, 64, 128], P(None, 'lev', 'tile'), may hold values from -6 to 6
- control_ens: float32 [2, 128, 64, 128], P(None, 'lev', 'tile'), may hold values from -6 to 6
- ens_perts: bfloat16 [2, 2, 128, 64, 128], P(None, None, 'lev', 'tile'), may hold values from -2.5 to 2.5
- band_sqrt: float32 [8, 2, 128, 128], P('tile', None, 'lev'), may hold values from -1 to 2
- band_owner: int32 [8], replicated, may hold values from 0 to 7, each once
- scale_class: int32 [64, 128], P('tile'), may hold values from 0 to 7
- static_scales: float32 [8], replicated, may hold values from 0.5 to 4
- local_scales: float32 [8], replicated, may hold values from 1 to 8
- obs_source: int32 [4096, 1], P('tile'), may hold values from 0 to 7; in each aligned block of 512 rows (0 to 511, 512 to 1023, ...) at most 256 rows name the same one
- obs_column: int32 [4096], P('tile'), may hold values from 0 to 1023
- obs_jac: float32 [8, 128, 2, 128], P('tile', None, None, 'lev'), may hold values from -0.375 to 0.375
- innovation: float32 [128, 4096], P(None, 'tile'), may hold values from -6 to 6
- obs_weight: float32 [128, 4096], P(None, 'tile'), may hold values from 0.2 to 5
Outputs:
- analysis_increment: float32 [2, 128, 64, 128], P(None, 'lev', 'tile')
- final_static: float32 [2, 128, 64, 128], P(None, 'lev', 'tile')
- final_ens: float32 [2, 128, 64, 128], P(None, 'lev', 'tile')
Inputs may be any that keep to these rules, and one draw needn't show every extreme that they name: `obs_source`: within each tile's block of 512 observations at most 256 name the same source tile, and some source tile is named exactly 256 times in some block. `band_owner`: each slot is named once.
All inputs are finite; a program needn't handle non-finite values.
Results may differ from a plain program's by a relative error of at most 0.0003.
Values sent between devices are 32-bit elements; how exact they have to be, the bound alone decides.
A program may use at most 64 MiB of HBM per device.

v0:
```python
import functools

import jax
import jax.numpy as jnp
from jax import lax
from jax.experimental import pallas as pl
from jax.experimental.pallas import tpu as pltpu
from jax.sharding import PartitionSpec as P

NSWEEP = 4
ITERS = 2

beta_static = 0.8
beta_ensemble = 0.6
step_length = 0.3
highest = lax.Precision.HIGHEST
MESH = pl.DeviceIdType.MESH
GROUP = 4
vmem = pl.BlockSpec(memory_space=pltpu.VMEM)


def beside(value, axis, dim, width):
    peers, length = lax.axis_size(axis), value.shape[dim]
    up = [(i, (i + 1) % peers) for i in range(peers)]
    down = [(j, i) for i, j in up]
    before = lax.ppermute(lax.slice_in_dim(value, length - width, length, axis=dim), axis, up)
    after = lax.ppermute(lax.slice_in_dim(value, 0, width, axis=dim), axis, down)
    return before, after


def padded(value, dim, width):
    before, after = beside(value, "tile", dim, width)
    return jnp.concatenate([before, value, after], axis=dim)


def split2(value):
    high = lax.reduce_precision(value, 8, 7)
    return high.astype(jnp.bfloat16), (value - high).astype(jnp.bfloat16)


def greet(peers):
    barrier = pltpu.get_barrier_semaphore()
    for peer in peers:
        pl.semaphore_signal(barrier, inc=1, device_id=peer, device_id_type=MESH)
    pl.semaphore_wait(barrier, len(peers))


def tile_peers():
    tiles, me = lax.axis_size("tile"), lax.axis_index("tile")
    return {"tile": lax.rem(me + tiles - 1, tiles)}, {"tile": lax.rem(me + 1, tiles)}


def lev_peers():
    me = lax.axis_index("lev")
    core = lax.rem(me, 2)
    return me, me + 1 - 2 * core, me + 2 - 4 * (me // 2)


def halo_copies(field, halo, index, send, recv):
    left, right = tile_peers()
    half = NSWEEP
    copies = []
    for side, peer in ((0, left), (1, right)):
        part = pl.ds(side * half, half)
        copies.append(
            pltpu.make_async_remote_copy(
                src_ref=field.at[:, part, :],
                dst_ref=halo.at[index, :, part, :],
                send_sem=send.at[index, side],
                recv_sem=recv.at[index, side],
                device_id=peer,
                device_id_type=MESH,
            )
        )
    return copies


def spread_copies(full, var, send, recv):
    me, core_peer, chip_peer = lev_peers()
    plan = ((me, core_peer), (me, chip_peer), (chip_peer, core_peer))
    return [
        pltpu.make_async_remote_copy(
            src_ref=full.at[block, var],
            dst_ref=full.at[block, var],
            send_sem=send.at[var, kind],
            recv_sem=recv.at[var, kind],
            device_id={"lev": peer},
            device_id_type=MESH,
        )
        for kind, (block, peer) in enumerate(plan)
    ]


def shifted(value):
    lons, lats = value.shape[1:]
    return (
        pltpu.roll(value, lons - 1, 1),
        pltpu.roll(value, 1, 1),
        pltpu.roll(value, lats - 1, 2),
        pltpu.roll(value, 1, 2),
    )


def neighbours(value, weights):
    east, west, north, south = shifted(value)
    return weights[0] * east + weights[1] * west + (weights[2] * north + weights[3] * south)


def kind_weights(w_ref, kind):
    return [w_ref[kind, i][None] for i in range(5)]


def over_rows(levels, body):
    def step(i, carry):
        body(pl.ds(pl.multiple_of(i * GROUP, GROUP), GROUP))
        return carry

    lax.fori_loop(0, levels // GROUP, step, 0)


def forward_rows(source, weights):
    current = source
    for sweep in range(NSWEEP):
        current = weights[4] * (source + neighbours(current, weights))
    return current


def backward_rows(source, weights):
    total, carried = jnp.zeros_like(source), source
    for sweep in range(NSWEEP):
        scaled = weights[4] * carried
        total = total + scaled
        carried = neighbours(scaled, weights)
    return total + carried


def forward_kernel(spread, mixed, ensemble, perts, w_ref, out, halo, hsend, hrecv, lsend, lrecv):
    variables, levels, lons, _ = mixed.shape
    members = ensemble.shape[0]
    me, core_peer, chip_peer = lev_peers()
    greet(tile_peers() + (({"lev": core_peer}, {"lev": chip_peer}) if spread else ()))
    copies = [halo_copies(mixed.at[v], halo, v, hsend, hrecv) for v in range(variables)]
    copies += [
        halo_copies(ensemble.at[e], halo, variables + e, hsend, hrecv) for e in range(members)
    ]
    for pair in copies:
        for copy in pair:
            copy.start()
    block = out.at[me] if spread else out
    for field in range(variables + members):
        for copy in copies[field]:
            copy.wait_recv()
        static = field < variables
        weights = kind_weights(w_ref, 0 if static else 1)
        own = mixed.at[field] if static else ensemble.at[field - variables]

        def body(rows):
            value = jnp.concatenate([own[rows], halo[field, rows]], axis=1)
            result = forward_rows(value, weights)[:, :lons]
            if static:
                block[field, rows] = beta_static * result
            else:
                result = beta_ensemble * result
                for v in range(variables):
                    block[v, rows] += perts[field - variables, v, rows] * result

        over_rows(levels, body)
    if spread:
        plans = [spread_copies(out, v, lsend, lrecv) for v in range(variables)]
        finish_spread(plans, start=True)
    for pair in copies:
        for copy in pair:
            copy.wait_send()


def finish_spread(plans, start):
    if start:
        for plan in plans:
            plan[1].start()
            plan[0].start()
    for plan in plans:
        plan[1].wait_recv()
        plan[2].start()
    for plan in plans:
        plan[0].wait_recv()
        plan[2].wait_recv()
        for copy in plan:
            copy.wait_send()


def backward_kernel(
    gradient, ensemble, perts, w_ref, full, updated, source, halo, hsend, hrecv, lsend, lrecv
):
    variables, levels, lons, _ = gradient.shape
    members = ensemble.shape[0]
    me, core_peer, chip_peer = lev_peers()
    greet(tile_peers() + ({"lev": core_peer}, {"lev": chip_peer}))

    def mix(rows):
        parts = [gradient[v, rows] for v in range(variables)]
        for v in range(variables):
            source[v, rows] = beta_static * parts[v]
        for e in range(members):
            total = perts[e, 0, rows] * parts[0]
            for v in range(1, variables):
                total = total + perts[e, v, rows] * parts[v]
            source[variables + e, rows] = beta_ensemble * total

    over_rows(levels, mix)
    copies = [
        halo_copies(source.at[f], halo, f, hsend, hrecv) for f in range(variables + members)
    ]
    for pair in copies:
        for copy in pair:
            copy.start()
    plans = [spread_copies(full, v, lsend, lrecv) for v in range(variables)]
    for field in range(variables + members):
        for copy in copies[field]:
            copy.wait_recv()
        static = field < variables
        weights = kind_weights(w_ref, 0 if static else 1)

        def body(rows):
            value = jnp.concatenate([source[field, rows], halo[field, rows]], axis=1)
            result = backward_rows(value, weights)[:, :lons]
            if static:
                full[me, field, rows] = result
            else:
                held = ensemble[field - variables, rows]
                updated[field - variables, rows] = held - step_length * (held + result)

        over_rows(levels, body)
        if static:
            plans[field][1].start()
            plans[field][0].start()
    finish_spread(plans, start=False)
    for pair in copies:
        for copy in pair:
            copy.wait_send()


def exchange_kernel(matrix, jacobian, payload, matrices, jacobians, arrived, send, recv):
    tiles, me = lax.axis_size("tile"), lax.axis_index("tile")
    barrier = pltpu.get_barrier_semaphore()

    def signal(offset, carry):
        peer = lax.rem(me + offset, tiles)
        pl.semaphore_signal(barrier, inc=1, device_id={"tile": peer}, device_id_type=MESH)
        return carry

    lax.fori_loop(1, tiles, signal, 0)
    pl.semaphore_wait(barrier, tiles - 1)

    def copies(offset):
        peer = lax.rem(me + offset, tiles)
        pairs = (
            (matrix, matrices.at[me]),
            (jacobian, jacobians.at[me]),
            (payload.at[peer], arrived.at[me]),
        )
        return [
            pltpu.make_async_remote_copy(
                src_ref=src,
                dst_ref=dst,
                send_sem=send.at[k, offset],
                recv_sem=recv.at[k, offset],
                device_id={"tile": peer},
                device_id_type=MESH,
            )
            for k, (src, dst) in enumerate(pairs)
        ]

    def begin(offset, carry):
        for copy in copies(offset):
            copy.start()
        return carry

    lax.fori_loop(1, tiles, begin, 0)
    matrices[me] = matrix[...]
    jacobians[me] = jacobian[...]
    arrived[me] = payload[me]

    def finish(offset, carry):
        for copy in copies(offset):
            copy.wait()
        return carry

    lax.fori_loop(1, tiles, finish, 0)


def call(kernel, name, identity, shapes, scratch, *operands):
    many = isinstance(shapes, list)
    result = pl.pallas_call(
        kernel,
        name=name,
        out_shape=shapes if many else [shapes],
        in_specs=[vmem] * len(operands),
        out_specs=[vmem] * (len(shapes) if many else 1),
        scratch_shapes=scratch,
        compiler_params=pltpu.CompilerParams(
            collective_id=identity, has_side_effects=True, vmem_limit_bytes=40 * 2**20
        ),
    )(*operands)
    return result if many else result[0]


def on_device(
    control_static,
    control_ens,
    ens_perts,
    band_sqrt,
    band_owner,
    scale_class,
    static_scales,
    local_scales,
    obs_source,
    obs_column,
    obs_jac,
    innovation,
    obs_weight,
):
    tiles = lax.axis_size("tile")
    levs = lax.axis_size("lev")
    lev_index = lax.axis_index("lev")
    variables, levels, lons, lats = control_static.shape
    members = control_ens.shape[0]
    all_levels = band_sqrt.shape[3]
    bands = band_owner.shape[0]
    height = lats // bands
    classes = static_scales.shape[0]
    columns = lons * lats
    channels = obs_jac.shape[1]
    obs_total = obs_column.shape[0]
    capacity = max(2, 4 * obs_total // tiles)
    share = channels // levs

    tables = jnp.stack([static_scales, local_scales])
    marks = (
        scale_class[None] == lax.broadcasted_iota(jnp.int32, (classes, lons, lats), 0)
    ).astype(jnp.float32)
    kappas = jnp.sum(tables[:, :, None, None] * marks[None], axis=1)
    wide_kappas = padded(kappas, 1, NSWEEP + 1)
    centre = wide_kappas[:, 1:-1]
    eastward = 0.5 * (centre + wide_kappas[:, 2:])
    westward = 0.5 * (wide_kappas[:, :-2] + centre)
    interior = 0.5 * (centre[:, :, :-1] + centre[:, :, 1:])
    edge_zero = jnp.zeros((2, centre.shape[1], 1), jnp.float32)
    northward = jnp.concatenate([interior, edge_zero], axis=2)
    southward = jnp.concatenate([edge_zero, interior], axis=2)
    inverse_diag = 1.0 / (1.0 + eastward + westward + northward + southward)
    weights = (eastward, westward, northward, southward, inverse_diag)
    wide_weights = jnp.roll(jnp.stack(weights, axis=1), -NSWEEP, axis=2)

    source = obs_source[:, 0]
    source_marks = source[:, None] == lax.broadcasted_iota(jnp.int32, (obs_total, tiles), 1)
    earlier = (
        lax.broadcasted_iota(jnp.int32, (obs_total, obs_total), 1)
        < lax.broadcasted_iota(jnp.int32, (obs_total, obs_total), 0)
    ).astype(jnp.bfloat16)
    before = jnp.dot(earlier, source_marks.astype(jnp.bfloat16), preferred_element_type=jnp.float32)
    slot = jnp.sum(jnp.where(source_marks, before, 0.0), axis=1).astype(jnp.int32)
    place = source * capacity + slot
    place_marks = (
        place[:, None] == lax.broadcasted_iota(jnp.int32, (obs_total, tiles * capacity), 1)
    ).astype(jnp.float32)
    own_share = lambda value: lax.dynamic_slice_in_dim(value, lev_index * share, share, axis=0)
    payload = jnp.concatenate(
        [
            own_share(obs_weight),
            own_share(innovation),
            jnp.broadcast_to(obs_column.astype(jnp.float32)[None], (8, obs_total)),
        ],
        axis=0,
    )
    outgoing = jnp.dot(payload, place_marks, precision=highest)
    outgoing = outgoing.reshape(payload.shape[0], tiles, capacity).transpose(1, 0, 2)
    own_jac = obs_jac[0].reshape(channels, variables * levels)
    shape = lambda *dims: jax.ShapeDtypeStruct(dims, jnp.float32)
    own_rows, jacs, arrived = call(
        exchange_kernel, "exchange", 0,
        [shape(tiles, *band_sqrt.shape[1:]), shape(tiles, *own_jac.shape), shape(*outgoing.shape)],
        [pltpu.SemaphoreType.DMA((3, tiles)), pltpu.SemaphoreType.DMA((3, tiles))],
        band_sqrt[0], own_jac, outgoing,
    )
    arrived = arrived.transpose(1, 0, 2).reshape(payload.shape[0], tiles * capacity)
    slots = tiles * capacity
    seen = arrived[2 * share].astype(jnp.int32)
    column_marks = (
        lax.broadcasted_iota(jnp.int32, (columns, slots), 0) == seen[None]
    ).astype(jnp.bfloat16)
    pair = lax.all_gather(arrived[:2 * share], "lev", axis=0, tiled=True)
    pair = pair.reshape(levs, 2, share, tiles, capacity).transpose(1, 3, 0, 2, 4)
    pair = pair.reshape(2, tiles, channels, capacity)
    slot_weight, slot_innovation = pair[0], pair[1]

    all_jacs = lax.all_gather(jacs, "lev", axis=2, tiled=True)

    own_rows = jnp.take(own_rows, band_owner, axis=0)
    roots = lax.all_gather(own_rows, "lev", axis=2, tiled=True)
    own_columns = lax.dynamic_slice_in_dim(roots, lev_index * levels, levels, axis=3)
    squares = jnp.einsum("bvlm,bvkm->bvlk", own_rows, roots, precision=highest)
    update = jnp.concatenate([own_columns.transpose(0, 1, 3, 2), squares], axis=2)

    def vertical(matrices, full):
        shaped = full.reshape(variables, all_levels, lons, bands, height)
        result = jnp.einsum("bvlm,vmxbr->vlxbr", matrices, shaped, precision=highest)
        return result.reshape(variables, matrices.shape[2], lons, lats)

    perts = ens_perts.astype(jnp.float32)

    fields = variables + members
    halo = pltpu.VMEM((fields, levels, lons, lats), jnp.float32)
    halo_sems = [pltpu.SemaphoreType.DMA((fields, 2))] * 2
    lev_sems = [pltpu.SemaphoreType.DMA((variables, 3))] * 2
    block = (variables, levels, lons, lats)

    def increment(mixed, ensemble, spread):
        return call(
            functools.partial(forward_kernel, spread), "forward", 1 if spread else 2,
            shape(levs, *block) if spread else shape(*block),
            [halo] + halo_sems + lev_sems, mixed, ensemble, perts, wide_weights,
        )

    static, ensemble = control_static, control_ens
    mixed = vertical(own_rows, lax.all_gather(static, "lev", axis=1, tiled=True))
    for iteration in range(ITERS):
        full = increment(mixed, ensemble, True).reshape(levs * variables * levels, columns)
        high, low = split2(full)
        picked = jnp.dot(jnp.concatenate([high, low], axis=0), column_marks,
                         preferred_element_type=jnp.float32)
        picked = (picked[:full.shape[0]] + picked[full.shape[0]:]).reshape(-1, tiles, capacity)
        observed = jnp.einsum("tcj,jto->tco", all_jacs, picked, precision=highest)
        weighted = slot_weight * (observed - slot_innovation)
        pulled = jnp.einsum("tcj,tco->jto", jacs, weighted, precision=highest)
        pulled = pulled.reshape(-1, slots)
        high, low = split2(pulled)
        gradient = lax.dot_general(
            jnp.concatenate([high, low], axis=0), column_marks, (((1,), (1,)), ((), ())),
            preferred_element_type=jnp.float32,
        )
        gradient = gradient[:pulled.shape[0]] + gradient[pulled.shape[0]:]
        gradient = gradient.reshape(control_static.shape)
        full, ensemble = call(
            backward_kernel, "backward", 3, [shape(levs, *block), shape(*control_ens.shape)],
            [halo, halo] + halo_sems + lev_sems, gradient, ensemble, perts, wide_weights,
        )
        full = full.transpose(1, 0, 2, 3, 4).reshape(variables, all_levels, lons, lats)
        steps = vertical(update, full)
        static = static - step_length * (static + steps[:, :levels])
        mixed = mixed - step_length * (mixed + steps[:, levels:])
    return (increment(mixed, ensemble, False), static, ensemble)


def solution(mesh):
    return jax.shard_map(
        on_device,
        mesh=mesh,
        in_specs=(
            P(None, "lev", "tile", None),
            P(None, "lev", "tile", None),
            P(None, None, "lev", "tile", None),
            P("tile", None, "lev", None),
            P(),
            P("tile", None),
            P(),
            P(),
            P("tile", None),
            P("tile"),
            P("tile", None, None, "lev"),
            P(None, "tile"),
            P(None, "tile"),
        ),
        out_specs=(
            P(None, "lev", "tile", None),
            P(None, "lev", "tile", None),
            P(None, "lev", "tile", None),
        ),
        check_vma=False,
    )
```

profile of v0, /device:TPU:0, one launch (start us, length us, event | category | flops | bytes accessed | tf_op | source)
XLA Modules:
  0.0 266.5 jit_solution(6745843596335725420)
XLA Ops:
  13.1 1.7 fusion.8
  14.9 28.6 %exchange.1 = (f32[8,2,32,128]{3,2,1,0:T(8,128)S(1)}, f32[8,128,64]{2,1,0:T(8,128)S(1)}, f32[8,72,256]{2,1,0:T(8,128)S(1)}) custom-call(f32[2,32,128]{2,1,0:T(8,128)S(1)} %bitcast.130, f32[128,64]{1,0:T(8,128)S(1)} %copy.105.jacobian, f32[8,72,256]{2,1,0:T(8,128)S(1)} %bitcast.123), custom_call_target="tpu_custom_call" | custom-call | tf_op jit(solution)/shard_map/exchange/pallas_call | solution.py:293
  46.2 2.7 %collective-permute-start = (f32[2,5,128]{2,1,0:T(8,128)S(1)}, f32[2,5,128]{2,1,0:T(8,128)S(1)}, u32[]{:S(2)}, u32[]{:S(2)}) collective-permute-start(f32[2,5,128]{2,1,0:T(8,128)S(1)} %get-tuple-element.31), channel_id=1, source_target_pairs={{0,4},{4,8},{8,12},{12,16},{16,20},{20,24},{24,28},{28,0},{1,5},{5... | collective-permute-start | bytes 15368 | tf_op jit(solution)/shard_map/ppermute | solution.py:26
  48.9 9.0 %collective-permute-start.1 = (f32[2,5,128]{2,1,0:T(8,128)S(1)}, f32[2,5,128]{2,1,0:T(8,128)S(1)}, u32[]{:S(2)}, u32[]{:S(2)}) collective-permute-start(f32[2,5,128]{2,1,0:T(8,128)S(1)} %get-tuple-element.32), channel_id=1, source_target_pairs={{4,0},{8,4},{12,8},{16,12},{20,16},{24,20},{28,24},{0,28},{5,1},{9... | collective-permute-start | bytes 15368 | tf_op jit(solution)/shard_map/ppermute | solution.py:27
  63.5 33.1 %forward.3 = f32[4,2,32,8,128]{4,3,2,1,0:T(8,128)S(1)} custom-call(f32[2,32,8,128]{3,2,1,0:T(8,128)S(1)} %copy.131.mixed, f32[2,32,8,128]{3,2,1,0:T(8,128)S(1)} %copy-done, f32[2,2,32,8,128]{4,3,2,1,0:T(8,128)S(1)} %convert_element_type.67.perts, f32[2,5,16,128]{3,2,1,0:T(8,128)S(1)} %pad_maximum_fusion.w_ref), custom_call_target="tpu_custom_call" | custom-call | tf_op jit(solution)/shard_map/forward/pallas_call | solution.py:293
  96.6 3.3 %fusion.74 = f32[8,2,32,128]{2,3,1,0:T(8,128)} fusion(f32[8,2,32,128]{3,2,1,0:T(8,128)S(1)} %copy-done.9, f32[8,2,128,128]{3,2,1,0:T(8,128)} %all-gather.11.cloned.1.call-done), kind=kOutput, calls=%fused_computation.117 | convolution fusion | flops 100663296 | bytes 1572864 | tf_op jit(solution)/shard_map/bvlm,bvkm->bvlk/dot_general | solution.py:401
  101.5 2.4 fusion.3
  105.6 2.5 copy.165
  110.0 8.1 %all-gather.9.cloned.1.call-done = f32[8,128,256]{1,0,2:T(8,128)} async-done(((f32[8,128,64]{1,0,2:T(8,128)}), f32[8,128,256]{1,0,2:T(8,128)}) %all-gather.9.cloned.1.call-update) | async-done | bytes 1048592 | tf_op jit(solution)/shard_map/all_gather | solution.py:396
  118.1 4.2 %fusion.25 = f32[8,128,256]{2,1,0:T(8,128)S(1)} fusion(f32[8,128,256]{2,1,0:T(8,128)} %bitcast.135, f32[8,128,256]{2,1,0:T(8,128)S(1)} %bitcast.133, f32[32,8,8,256]{3,2,1,0:T(8,128)} %bitcast.137, f32[8,128,256]{1,0,2:T(8,128)} %all-gather.9.cloned.1.call-done), kind=kOutput, calls=%fused_computation.31 | convolution fusion | flops 805830656 | bytes 6291456 | tf_op jit(solution)/shard_map/tcj,jto->tco/dot_general | solution.py:432
  123.6 1.9 fusion.2
  125.6 23.0 %backward.2 = (f32[4,2,32,8,128]{4,3,2,1,0:T(8,128)S(1)}, f32[2,32,8,128]{3,2,1,0:T(8,128)S(1)}) custom-call(f32[2,32,8,128]{3,2,1,0:T(8,128)S(1)} %bitcast.127, f32[2,32,8,128]{3,2,1,0:T(8,128)S(1)} %copy-done, f32[2,2,32,8,128]{4,3,2,1,0:T(8,128)S(1)} %convert_element_type.67.perts, f32[2,5,16,128]{3,2,1,0:T(8,128)S(1)} %pad_maximum_fusion.w_ref), custom_call_target="tpu_custom_call" | custom-call | tf_op jit(solution)/shard_map/backward/pallas_call | solution.py:293
  148.6 2.9 %copy.124 = f32[2,4,32,8,128]{2,1,4,3,0:T(4,128)} copy(f32[2,4,32,8,128]{4,3,2,0,1:T(8,128)S(1)} %bitcast.125) | data formatting | bytes 2097152 | tf_op jit(solution)/shard_map/transpose | solution.py:447
  151.5 4.6 %reshape_reshape.6 = f32[2,128,8,8,16]{1,4,3,2,0:T(8,128)} reshape(f32[2,4,32,8,128]{2,1,4,3,0:T(4,128)} %copy.124) | data formatting | bytes 2097152 | tf_op jit(solution)/shard_map/reshape;reshape | solution.py:405
  156.1 2.8 %convolution_bitcast_fusion.1 = f32[2,64,8,8,16]{1,4,2,3,0:T(8,128)S(1)} fusion(f32[2,128,8,8,16]{1,4,3,2,0:T(8,128)} %reshape_reshape.6, f32[8,2,32,128]{2,3,1,0:T(8,128)} %fusion.74, f32[8,2,32,128]{2,3,1,0:T(8,128)S(1)} %copy-done.2), kind=kOutput, calls=%fused_computation.28 | convolution fusion | flops 201457664 | bytes 2097152 | tf_op jit(solution)/shard_map/bvlm,vmxbr->vlxbr/dot_general | solution.py:406
  162.3 27.3 %forward.4 = f32[4,2,32,8,128]{4,3,2,1,0:T(8,128)S(1)} custom-call(f32[2,32,8,128]{3,2,1,0:T(8,128)S(1)} %multiply_subtract_fusion.2.mixed, f32[2,32,8,128]{3,2,1,0:T(8,128)S(1)} %get-tuple-element.14.ensemble, f32[2,2,32,8,128]{4,3,2,1,0:T(8,128)S(1)} %convert_element_type.67.perts, f32[2,5,16,128]{3,2,1,0:T(8,128)S(1)} %pad_maximum_fusion.w_ref), custom_call_target="tpu_custom_call" | custom-call | tf_op jit(solution)/shard_map/forward/pallas_call | solution.py:293
  189.9 2.4 fusion.1
  194.2 2.0 fusion.22
  197.5 1.9 fusion
  199.5 24.3 %backward.3 = (f32[4,2,32,8,128]{4,3,2,1,0:T(8,128)S(1)}, f32[2,32,8,128]{3,2,1,0:T(8,128)S(1)}) custom-call(f32[2,32,8,128]{3,2,1,0:T(8,128)S(1)} %bitcast.126, f32[2,32,8,128]{3,2,1,0:T(8,128)S(1)} %get-tuple-element.14.ensemble, f32[2,2,32,8,128]{4,3,2,1,0:T(8,128)S(1)} %convert_element_type.67.perts, f32[2,5,16,128]{3,2,1,0:T(8,128)S(1)} %pad_maximum_fusion.w_ref), custom_call_target="tpu_custom_call" | custom-call | tf_op jit(solution)/shard_map/backward/pallas_call | solution.py:293
  223.8 2.7 %copy.136 = f32[2,4,32,8,128]{2,1,4,3,0:T(4,128)} copy(f32[2,4,32,8,128]{4,3,2,0,1:T(8,128)S(1)} %bitcast.124) | data formatting | bytes 2097152 | tf_op jit(solution)/shard_map/transpose | solution.py:447
  226.5 4.6 %reshape_reshape.7 = f32[2,128,8,8,16]{1,4,3,2,0:T(8,128)} reshape(f32[2,4,32,8,128]{2,1,4,3,0:T(4,128)} %copy.136) | data formatting | bytes 2097152 | tf_op jit(solution)/shard_map/reshape;reshape | solution.py:405
  231.1 2.8 %convolution_bitcast_fusion = f32[2,64,8,8,16]{1,4,2,3,0:T(8,128)S(1)} fusion(f32[2,128,8,8,16]{1,4,3,2,0:T(8,128)} %reshape_reshape.7, f32[8,2,32,128]{2,3,1,0:T(8,128)} %fusion.74, f32[8,2,32,128]{2,3,1,0:T(8,128)S(1)} %copy-done.3), kind=kOutput, calls=%fused_computation.27 | convolution fusion | flops 201457664 | bytes 2097152 | tf_op jit(solution)/shard_map/bvlm,vmxbr->vlxbr/dot_general | solution.py:406
  237.3 20.4 %forward.5 = f32[2,32,8,128]{3,2,1,0:T(8,128)S(1)} custom-call(f32[2,32,8,128]{3,2,1,0:T(8,128)S(1)} %multiply_subtract_fusion.1.mixed, f32[2,32,8,128]{3,2,1,0:T(8,128)S(1)} %get-tuple-element.40.ensemble, f32[2,2,32,8,128]{4,3,2,1,0:T(8,128)S(1)} %convert_element_type.67.perts, f32[2,5,16,128]{3,2,1,0:T(8,128)S(1)} %pad_maximum_fusion.w_ref), custom_call_target="tpu_custom_call" | custom-call | tf_op jit(solution)/shard_map/forward/pallas_call | solution.py:293
  (113 shorter events, 32.8 us)
Async XLA Ops:
  7.2 7.8 %copy-start.1 = (f32[1,2,32,128]{3,2,1,0:T(8,128)S(1)}, f32[1,2,32,128]{3,2,1,0:T(8,128)}, u32[]{:S(2)}) copy-start(f32[1,2,32,128]{3,2,1,0:T(8,128)} %param.16) | copy-start | bytes 98308
  7.2 52.7 %all-gather.5.cloned.1.call-start = ((), (), s32[]{:S(2)}) async-start(), calls=%async_computation | async-start | bytes 1310720 | tf_op jit(solution)/shard_map/all_gather | solution.py:425
  8.9 34.6 %copy-start.15 = (s32[8]{0:T(128)S(1)}, s32[8]{0:T(128)}, u32[]{:S(2)}) copy-start(s32[8]{0:T(128)} %param.17) | copy-start | bytes 100
  8.9 87.7 %all-gather.11.cloned.1.call-start = ((), (), s32[]{:S(2)}) async-start(), calls=%async_computation.3 | async-start | bytes 1310720 | tf_op jit(solution)/shard_map/all_gather | solution.py:399
  43.5 2.5 copy-start.13
  43.5 2.5 copy-start.14
  43.5 2.5 copy-start.12
  44.9 13.9 %copy-start.11 = (bf16[2,2,32,8,128]{4,3,2,1,0:T(8,128)(2,1)S(1)}, bf16[2,2,32,8,128]{4,3,2,1,0:T(8,128)(2,1)}, u32[]{:S(2)}) copy-start(bf16[2,2,32,8,128]{4,3,2,1,0:T(8,128)(2,1)} %param.15) | copy-start | bytes 786436
  45.0 60.6 %all-gather.7.cloned.1.call-start = ((), (), s32[]{:S(2)}) async-start(), calls=%async_computation.1 | async-start | bytes 2621440 | tf_op jit(solution)/shard_map/all_gather | solution.py:391
  46.0 72.1 %all-gather.9.cloned.1.call-start = ((), (), s32[]{:S(2)}) async-start(), calls=%async_computation.2 | async-start | bytes 1310720 | tf_op jit(solution)/shard_map/all_gather | solution.py:396
  46.2 13.3 %collective-permute-start = (f32[2,5,128]{2,1,0:T(8,128)S(1)}, f32[2,5,128]{2,1,0:T(8,128)S(1)}, u32[]{:S(2)}, u32[]{:S(2)}) collective-permute-start(f32[2,5,128]{2,1,0:T(8,128)S(1)} %get-tuple-element.31), channel_id=1, source_target_pairs={{0,4},{4,8},{8,12},{12,16},{16,20},{20,24},{24,28},{28,0},{1,5},{5... | collective-permute-start | bytes 15368 | tf_op jit(solution)/shard_map/ppermute | solution.py:26
  48.9 10.6 %collective-permute-start.1 = (f32[2,5,128]{2,1,0:T(8,128)S(1)}, f32[2,5,128]{2,1,0:T(8,128)S(1)}, u32[]{:S(2)}, u32[]{:S(2)}) collective-permute-start(f32[2,5,128]{2,1,0:T(8,128)S(1)} %get-tuple-element.32), channel_id=1, source_target_pairs={{4,0},{8,4},{12,8},{16,12},{20,16},{24,20},{28,24},{0,28},{5,1},{9... | collective-permute-start | bytes 15368 | tf_op jit(solution)/shard_map/ppermute | solution.py:27
  62.5 1.0 copy-start
  62.7 34.0 %copy-start.9 = (f32[8,2,32,128]{3,2,1,0:T(8,128)S(1)}, f32[8,2,32,128]{3,2,1,0:T(8,128)}, u32[]{:S(2)}) copy-start(f32[8,2,32,128]{3,2,1,0:T(8,128)} %broadcast_select_fusion) | copy-start | bytes 786436
  96.6 3.3 %copy-start.7 = (f32[8,2,128,128]{3,2,1,0:T(8,128)S(1)}, f32[8,2,128,128]{3,2,1,0:T(8,128)}, u32[]{:S(2)}) copy-start(f32[8,2,128,128]{3,2,1,0:T(8,128)} %all-gather.11.cloned.1.call-done) | copy-start | bytes 3145732
  108.6 13.7 %copy-start.4 = (f32[1,8,4,32,256]{4,3,2,1,0:T(8,128)}, f32[1,8,4,32,256]{4,3,2,1,0:T(8,128)S(1)}, u32[]{:S(2)}) copy-start(f32[1,8,4,32,256]{4,3,2,1,0:T(8,128)S(1)} %copy.121) | copy-start | bytes 3145732
  151.5 4.6 %copy-start.2 = (f32[8,2,32,128]{2,3,1,0:T(8,128)S(1)}, f32[8,2,32,128]{2,3,1,0:T(8,128)}, u32[]{:S(2)}) copy-start(f32[8,2,32,128]{2,3,1,0:T(8,128)} %dynamic-slice_bitcast_fusion) | copy-start | bytes 786436
  192.3 1.2 copy-start.5
  192.3 1.5 copy-start.6
  192.3 1.8 copy-start.8
  226.5 4.6 %copy-start.3 = (f32[8,2,32,128]{2,3,1,0:T(8,128)S(1)}, f32[8,2,32,128]{2,3,1,0:T(8,128)}, u32[]{:S(2)}) copy-start(f32[8,2,32,128]{2,3,1,0:T(8,128)} %dynamic-slice_bitcast_fusion) | copy-start | bytes 786436
  235.4 22.4 %copy-start.10 = (f32[2,32,8,128]{3,2,1,0:T(8,128)S(1)}, f32[2,32,8,128]{3,2,1,0:T(8,128)}, u32[]{:S(2)}) copy-start(f32[2,32,8,128]{3,2,1,0:T(8,128)} %param.13) | copy-start | bytes 786436
Sparse Core Ops, SparseCore 0:
  10.1 19.4 all-gather.4
  45.1 25.0 all-gather.10
  71.8 28.4 all-gather.6
  102.3 15.7 all-gather.8
where the time goes:
time: 267 us; the launch traced here: 266 us
  Pallas kernels  157 us (59%)
  local copies, waits for them, and re-layouts  38.7 us (14%)
  matrix products  29.9 us (11%)
  between operations  14.4 us (5%)
  starting transfers between devices  11.9 us (4%)
  waiting for transfers between devices  8.82 us (3%)
  other arithmetic  6.06 us (2%)
    pallas_call x6, Pallas kernels, call(): pl.pallas_call(kernel, name=name, out_shape=shapes if many else [shapes],...  157 us
    unnamed x45, local copies, waits for them, and re-layouts  11.6 us
    another operation x2, local copies, waits for them, and re-layouts, vertical(): shaped = full.reshape(variables, all_levels, lons, bands, height)  9.25 us
    ppermute x1, starting transfers between devices, beside(): lax.ppermute(lax.slice_in_dim(value, 0, width, axis=dim), axis, down)  9.03 us
    all_gather x1, waiting for transfers between devices, on_device(): all_jacs = lax.all_gather(jacs, 'lev', axis=2, tiled=True)  8.12 us
    dot_general x3, matrix products, vertical(): jnp.einsum('bvlm,vmxbr->vlxbr', matrices, shaped, precision=highest)  6.64 us
    dot_general x2, matrix products, on_device(): observed = jnp.einsum('tcj,jto->tco', all_jacs, picked, precision=highest)  6.2 us
    transpose x2, local copies, waits for them, and re-layouts, on_device(): full.transpose(1, 0, 2, 3, 4).reshape(variables, all_levels, lons, lats)  5.56 us
  transfers between devices with their start and end apart: 6, of which 2 were waited for; matrix products, arithmetic and copies ran while one was open for 10% of the time, Pallas kernels for 23%

commit v1 on v0

--- a/solution.py
+++ b/solution.py
@@ -15,22 +15,8 @@
 step_length = 0.3
 highest = lax.Precision.HIGHEST
 MESH = pl.DeviceIdType.MESH
-GROUP = 4
+GROUP = 8
 vmem = pl.BlockSpec(memory_space=pltpu.VMEM)
-
-
-def beside(value, axis, dim, width):
-    peers, length = lax.axis_size(axis), value.shape[dim]
-    up = [(i, (i + 1) % peers) for i in range(peers)]
-    down = [(j, i) for i, j in up]
-    before = lax.ppermute(lax.slice_in_dim(value, length - width, length, axis=dim), axis, up)
-    after = lax.ppermute(lax.slice_in_dim(value, 0, width, axis=dim), axis, down)
-    return before, after
-
-
-def padded(value, dim, width):
-    before, after = beside(value, "tile", dim, width)
-    return jnp.concatenate([before, value, after], axis=dim)
 
 
 def split2(value):
@@ -58,14 +44,13 @@
 
 def halo_copies(field, halo, index, send, recv):
     left, right = tile_peers()
-    half = NSWEEP
+    half, lons = NSWEEP, field.shape[0]
     copies = []
-    for side, peer in ((0, left), (1, right)):
-        part = pl.ds(side * half, half)
+    for side, peer, start in ((1, left, 0), (0, right, lons - half)):
         copies.append(
             pltpu.make_async_remote_copy(
-                src_ref=field.at[:, part, :],
-                dst_ref=halo.at[index, :, part, :],
+                src_ref=field.at[pl.ds(start, half)],
+                dst_ref=halo.at[index, pl.ds(side * half, half)],
                 send_sem=send.at[index, side],
                 recv_sem=recv.at[index, side],
                 device_id=peer,
@@ -91,23 +76,16 @@
     ]
 
 
-def shifted(value):
-    lons, lats = value.shape[1:]
-    return (
-        pltpu.roll(value, lons - 1, 1),
-        pltpu.roll(value, 1, 1),
-        pltpu.roll(value, lats - 1, 2),
-        pltpu.roll(value, 1, 2),
-    )
-
-
-def neighbours(value, weights):
-    east, west, north, south = shifted(value)
-    return weights[0] * east + weights[1] * west + (weights[2] * north + weights[3] * south)
+def neighbours(wide, weights):
+    lats = wide.shape[2]
+    inner = wide[1:-1]
+    return (weights[0] * wide[2:] + weights[1] * wide[:-2]) + (
+        weights[2] * pltpu.roll(inner, lats - 1, 2) + weights[3] * pltpu.roll(inner, 1, 2)
+    )
 
 
 def kind_weights(w_ref, kind):
-    return [w_ref[kind, i][None] for i in range(5)]
+    return lambda i, start, count: w_ref[kind, i, pl.ds(start, count)]
 
 
 def over_rows(levels, body):
@@ -118,24 +96,36 @@
     lax.fori_loop(0, levels // GROUP, step, 0)
 
 
+def widened(field, halo, index, rows):
+    half = NSWEEP
+    return jnp.concatenate(
+        [halo[index, :half, rows], field[:, rows], halo[index, half:, rows]], axis=0
+    )
+
+
 def forward_rows(source, weights):
     current = source
+    for sweep in range(1, NSWEEP + 1):
+        count = source.shape[0] - 2 * sweep
+        here = [weights(i, sweep, count) for i in range(5)]
+        current = here[4] * (source[sweep:sweep + count] + neighbours(current, here))
+    return current
+
+
+def backward_rows(source, weights):
+    lons = source.shape[0] - 2 * NSWEEP
+    total, carried = 0.0, source
     for sweep in range(NSWEEP):
-        current = weights[4] * (source + neighbours(current, weights))
-    return current
-
-
-def backward_rows(source, weights):
-    total, carried = jnp.zeros_like(source), source
-    for sweep in range(NSWEEP):
-        scaled = weights[4] * carried
-        total = total + scaled
-        carried = neighbours(scaled, weights)
+        count = source.shape[0] - 2 * sweep
+        scaled = weights(4, sweep, count) * carried
+        inner = NSWEEP - sweep
+        total = total + scaled[inner:inner + lons]
+        carried = neighbours(scaled, [weights(i, sweep + 1, count - 2) for i in range(4)])
     return total + carried
 
 
 def forward_kernel(spread, mixed, ensemble, perts, w_ref, out, halo, hsend, hrecv, lsend, lrecv):
-    variables, levels, lons, _ = mixed.shape
+    variables, _, levels, _ = mixed.shape
     members = ensemble.shape[0]
     me, core_peer, chip_peer = lev_peers()
     greet(tile_peers() + (({"lev": core_peer}, {"lev": chip_peer}) if spread else ()))
@@ -155,14 +145,13 @@
         own = mixed.at[field] if static else ensemble.at[field - variables]
 
         def body(rows):
-            value = jnp.concatenate([own[rows], halo[field, rows]], axis=1)
-            result = forward_rows(value, weights)[:, :lons]
+            result = forward_rows(widened(own, halo, field, rows), weights)
             if static:
-                block[field, rows] = beta_static * result
+                block[field, :, rows] = beta_static * result
             else:
                 result = beta_ensemble * result
                 for v in range(variables):
-                    block[v, rows] += perts[field - variables, v, rows] * result
+                    block[v, :, rows] += perts[field - variables, v, :, rows] * result
 
         over_rows(levels, body)
     if spread:
@@ -191,20 +180,20 @@
 def backward_kernel(
     gradient, ensemble, perts, w_ref, full, updated, source, halo, hsend, hrecv, lsend, lrecv
 ):
-    variables, levels, lons, _ = gradient.shape
+    variables, _, levels, _ = gradient.shape
     members = ensemble.shape[0]
     me, core_peer, chip_peer = lev_peers()
     greet(tile_peers() + ({"lev": core_peer}, {"lev": chip_peer}))
 
     def mix(rows):
-        parts = [gradient[v, rows] for v in range(variables)]
+        parts = [gradient[v, :, rows] for v in range(variables)]
         for v in range(variables):
-            source[v, rows] = beta_static * parts[v]
+            source[v, :, rows] = beta_static * parts[v]
         for e in range(members):
-            total = perts[e, 0, rows] * parts[0]
+            total = perts[e, 0, :, rows] * parts[0]
             for v in range(1, variables):
-                total = total + perts[e, v, rows] * parts[v]
-            source[variables + e, rows] = beta_ensemble * total
+                total = total + perts[e, v, :, rows] * parts[v]
+            source[variables + e, :, rows] = beta_ensemble * total
 
     over_rows(levels, mix)
     copies = [
@@ -221,13 +210,12 @@
         weights = kind_weights(w_ref, 0 if static else 1)
 
         def body(rows):
-            value = jnp.concatenate([source[field, rows], halo[field, rows]], axis=1)
-            result = backward_rows(value, weights)[:, :lons]
+            result = backward_rows(widened(source.at[field], halo, field, rows), weights)
             if static:
-                full[me, field, rows] = result
+                full[me, field, :, rows] = result
             else:
-                held = ensemble[field - variables, rows]
-                updated[field - variables, rows] = held - step_length * (held + result)
+                held = ensemble[field - variables, :, rows]
+                updated[field - variables, :, rows] = held - step_length * (held + result)
 
         over_rows(levels, body)
         if static:
@@ -239,7 +227,9 @@
             copy.wait_send()
 
 
-def exchange_kernel(matrix, jacobian, payload, matrices, jacobians, arrived, send, recv):
+def exchange_kernel(
+    matrix, jacobian, kappa, payload, matrices, jacobians, kappas, arrived, send, recv
+):
     tiles, me = lax.axis_size("tile"), lax.axis_index("tile")
     barrier = pltpu.get_barrier_semaphore()
 
@@ -256,6 +246,7 @@
         pairs = (
             (matrix, matrices.at[me]),
             (jacobian, jacobians.at[me]),
+            (kappa, kappas.at[me]),
             (payload.at[peer], arrived.at[me]),
         )
         return [
@@ -278,6 +269,7 @@
     lax.fori_loop(1, tiles, begin, 0)
     matrices[me] = matrix[...]
     jacobians[me] = jacobian[...]
+    kappas[me] = kappa[...]
     arrived[me] = payload[me]
 
     def finish(offset, carry):
@@ -286,6 +278,29 @@
         return carry
 
     lax.fori_loop(1, tiles, finish, 0)
+
+
+def vertical_kernel(full, matrices, static, mixed, new_static, new_mixed):
+    levs, variables, lons, levels, lats = full.shape
+    rows = 2 * levels
+    bands = matrices.shape[1] // rows
+    band = lax.broadcasted_iota(jnp.int32, (rows, lats), 1) // (lats // bands)
+
+    def step(x, carry):
+        for v in range(variables):
+            column = jnp.concatenate([full[block, v, x] for block in range(levs)], axis=0)
+            product = jnp.dot(
+                matrices[v], column, precision=highest, preferred_element_type=jnp.float32
+            )
+            kept = product[:rows]
+            for b in range(1, bands):
+                kept = jnp.where(band == b, product[b * rows:(b + 1) * rows], kept)
+            held, other = static[v, x], mixed[v, x]
+            new_static[v, x] = held - step_length * (held + kept[:levels])
+            new_mixed[v, x] = other - step_length * (other + kept[levels:])
+        return carry
+
+    lax.fori_loop(0, lons, step, 0)
 
 
 def call(kernel, name, identity, shapes, scratch, *operands):
@@ -298,7 +313,9 @@
         out_specs=[vmem] * (len(shapes) if many else 1),
         scratch_shapes=scratch,
         compiler_params=pltpu.CompilerParams(
-            collective_id=identity, has_side_effects=True, vmem_limit_bytes=40 * 2**20
+            collective_id=identity,
+            has_side_effects=identity is not None,
+            vmem_limit_bytes=40 * 2**20,
         ),
     )(*operands)
     return result if many else result[0]
@@ -339,17 +356,6 @@
         scale_class[None] == lax.broadcasted_iota(jnp.int32, (classes, lons, lats), 0)
     ).astype(jnp.float32)
     kappas = jnp.sum(tables[:, :, None, None] * marks[None], axis=1)
-    wide_kappas = padded(kappas, 1, NSWEEP + 1)
-    centre = wide_kappas[:, 1:-1]
-    eastward = 0.5 * (centre + wide_kappas[:, 2:])
-    westward = 0.5 * (wide_kappas[:, :-2] + centre)
-    interior = 0.5 * (centre[:, :, :-1] + centre[:, :, 1:])
-    edge_zero = jnp.zeros((2, centre.shape[1], 1), jnp.float32)
-    northward = jnp.concatenate([interior, edge_zero], axis=2)
-    southward = jnp.concatenate([edge_zero, interior], axis=2)
-    inverse_diag = 1.0 / (1.0 + eastward + westward + northward + southward)
-    weights = (eastward, westward, northward, southward, inverse_diag)
-    wide_weights = jnp.roll(jnp.stack(weights, axis=1), -NSWEEP, axis=2)
 
     source = obs_source[:, 0]
     source_marks = source[:, None] == lax.broadcasted_iota(jnp.int32, (obs_total, tiles), 1)
@@ -376,12 +382,32 @@
     outgoing = outgoing.reshape(payload.shape[0], tiles, capacity).transpose(1, 0, 2)
     own_jac = obs_jac[0].reshape(channels, variables * levels)
     shape = lambda *dims: jax.ShapeDtypeStruct(dims, jnp.float32)
-    own_rows, jacs, arrived = call(
+    own_rows, jacs, all_kappas, arrived = call(
         exchange_kernel, "exchange", 0,
-        [shape(tiles, *band_sqrt.shape[1:]), shape(tiles, *own_jac.shape), shape(*outgoing.shape)],
-        [pltpu.SemaphoreType.DMA((3, tiles)), pltpu.SemaphoreType.DMA((3, tiles))],
-        band_sqrt[0], own_jac, outgoing,
-    )
+        [shape(tiles, *band_sqrt.shape[1:]), shape(tiles, *own_jac.shape),
+         shape(tiles, *kappas.shape), shape(*outgoing.shape)],
+        [pltpu.SemaphoreType.DMA((4, tiles)), pltpu.SemaphoreType.DMA((4, tiles))],
+        band_sqrt[0], own_jac, kappas, outgoing,
+    )
+    me = lax.axis_index("tile")
+    beside = lambda step: lax.dynamic_index_in_dim(
+        all_kappas, lax.rem(me + step + tiles, tiles), keepdims=False
+    )
+    wide_kappas = jnp.concatenate(
+        [beside(-1)[:, -NSWEEP - 1:], kappas, beside(1)[:, :NSWEEP + 1]], axis=1
+    )
+    centre = wide_kappas[:, 1:-1]
+    eastward = 0.5 * (centre + wide_kappas[:, 2:])
+    westward = 0.5 * (wide_kappas[:, :-2] + centre)
+    interior = 0.5 * (centre[:, :, :-1] + centre[:, :, 1:])
+    edge_zero = jnp.zeros((2, centre.shape[1], 1), jnp.float32)
+    northward = jnp.concatenate([interior, edge_zero], axis=2)
+    southward = jnp.concatenate([edge_zero, interior], axis=2)
+    inverse_diag = 1.0 / (1.0 + eastward + westward + northward + southward)
+    weights = (eastward, westward, northward, southward, inverse_diag)
+    wide_weights = jnp.stack(weights, axis=1)[:, :, :, None]
+    wide_weights = jnp.broadcast_to(wide_weights, wide_weights.shape[:3] + (GROUP, lats))
+
     arrived = arrived.transpose(1, 0, 2).reshape(payload.shape[0], tiles * capacity)
     slots = tiles * capacity
     seen = arrived[2 * share].astype(jnp.int32)
@@ -400,19 +426,21 @@
     own_columns = lax.dynamic_slice_in_dim(roots, lev_index * levels, levels, axis=3)
     squares = jnp.einsum("bvlm,bvkm->bvlk", own_rows, roots, precision=highest)
     update = jnp.concatenate([own_columns.transpose(0, 1, 3, 2), squares], axis=2)
+    update = update.transpose(1, 0, 2, 3).reshape(variables, -1, all_levels)
 
     def vertical(matrices, full):
         shaped = full.reshape(variables, all_levels, lons, bands, height)
         result = jnp.einsum("bvlm,vmxbr->vlxbr", matrices, shaped, precision=highest)
         return result.reshape(variables, matrices.shape[2], lons, lats)
 
-    perts = ens_perts.astype(jnp.float32)
+    perts = ens_perts.transpose(0, 1, 3, 2, 4).astype(jnp.float32)
 
     fields = variables + members
-    halo = pltpu.VMEM((fields, levels, lons, lats), jnp.float32)
+    halo = pltpu.VMEM((fields, 2 * NSWEEP, levels, lats), jnp.float32)
     halo_sems = [pltpu.SemaphoreType.DMA((fields, 2))] * 2
     lev_sems = [pltpu.SemaphoreType.DMA((variables, 3))] * 2
-    block = (variables, levels, lons, lats)
+    source = pltpu.VMEM((fields, lons, levels, lats), jnp.float32)
+    block = (variables, lons, levels, lats)
 
     def increment(mixed, ensemble, spread):
         return call(
@@ -421,10 +449,13 @@
             [halo] + halo_sems + lev_sems, mixed, ensemble, perts, wide_weights,
         )
 
-    static, ensemble = control_static, control_ens
-    mixed = vertical(own_rows, lax.all_gather(static, "lev", axis=1, tiled=True))
+    turned = lambda value: value.transpose(0, 2, 1, 3)
+    static, ensemble = turned(control_static), turned(control_ens)
+    mixed = vertical(own_rows, lax.all_gather(control_static, "lev", axis=1, tiled=True))
+    mixed = turned(mixed)
     for iteration in range(ITERS):
-        full = increment(mixed, ensemble, True).reshape(levs * variables * levels, columns)
+        full = increment(mixed, ensemble, True).transpose(0, 1, 3, 2, 4)
+        full = full.reshape(levs * variables * levels, columns)
         high, low = split2(full)
         picked = jnp.dot(jnp.concatenate([high, low], axis=0), column_marks,
                          preferred_element_type=jnp.float32)
@@ -439,16 +470,16 @@
             preferred_element_type=jnp.float32,
         )
         gradient = gradient[:pulled.shape[0]] + gradient[pulled.shape[0]:]
-        gradient = gradient.reshape(control_static.shape)
+        gradient = turned(gradient.reshape(control_static.shape))
         full, ensemble = call(
-            backward_kernel, "backward", 3, [shape(levs, *block), shape(*control_ens.shape)],
-            [halo, halo] + halo_sems + lev_sems, gradient, ensemble, perts, wide_weights,
-        )
-        full = full.transpose(1, 0, 2, 3, 4).reshape(variables, all_levels, lons, lats)
-        steps = vertical(update, full)
-        static = static - step_length * (static + steps[:, :levels])
-        mixed = mixed - step_length * (mixed + steps[:, levels:])
-    return (increment(mixed, ensemble, False), static, ensemble)
+            backward_kernel, "backward", 3, [shape(levs, *block), shape(members, *block[1:])],
+            [source, halo] + halo_sems + lev_sems, gradient, ensemble, perts, wide_weights,
+        )
+        static, mixed = call(
+            vertical_kernel, "vertical", None, [shape(*block), shape(*block)], [],
+            full, update, static, mixed,
+        )
+    return tuple(turned(value) for value in (increment(mixed, ensemble, False), static, ensemble))
 
 
 def solution(mesh):

time: 267 us -> 237 us (0.89)
  local copies, waits for them, and re-layouts: 38.7 us -> 20.7 us
  waiting for transfers between devices: 8.82 us -> 23.5 us
  starting transfers between devices: 11.9 us -> 0.16 us
  Pallas kernels: 157 us -> 148 us
  matrix products: 29.9 us -> 23.6 us
    all_gather x1, waiting for transfers between devices: 0.02 us -> 20 us  [on_device(): roots = lax.all_gather(own_rows, 'lev', axis=2, tiled=True)]
    ppermute x2 -> x0, starting transfers between devices: 11.8 us -> none  [the longest x1 9.03 us: beside(): lax.ppermute(lax.slice_in_dim(value, 0, width, axis=dim), axis, down)]
    another operation x2 -> x1, local copies, waits for them, and re-layouts: 9.25 us -> 0.01 us  [on_device(): wide_weights = jnp.stack(weights, axis=1)[:, :, :, None]]
    pallas_call x6 -> x8, Pallas kernels: 157 us -> 148 us  [call(): pl.pallas_call(kernel, name=name, out_shape=shapes if many else [shapes],...]
    dot_general x3 -> x1, matrix products: 6.64 us -> 1.03 us  [vertical(): jnp.einsum('bvlm,vmxbr->vlxbr', matrices, shaped, precision=highest)]
    all_gather x1, waiting for transfers between devices: 8.12 us -> 3.43 us  [on_device(): all_jacs = lax.all_gather(jacs, 'lev', axis=2, tiled=True)]
    unnamed x45 -> x38, local copies, waits for them, and re-layouts: 11.6 us -> 8.58 us
    transpose x2 -> x3, local copies, waits for them, and re-layouts: 5.56 us -> 2.75 us  [the longest x1 1.54 us: on_device(): update = update.transpose(1, 0, 2, 3).reshape(variables, -1, all_levels)]
  transfers between devices with their start and end apart: 6 -> 4, of which waited for: 2 -> 2; matrix products, arithmetic and copies ran while one was open for 10% -> 12% of each run, Pallas kernels for 23% -> 23%
where the time goes in v1:
time: 237 us
  Pallas kernels  148 us (62%)
  matrix products  23.6 us (10%)
  waiting for transfers between devices  23.5 us (10%)
  local copies, waits for them, and re-layouts  20.7 us (9%)
  between operations  14.4 us (6%)
  other arithmetic  6.57 us (3%)
    pallas_call x8, Pallas kernels, call(): pl.pallas_call(kernel, name=name, out_shape=shapes if many else [shapes],...  148 us
    all_gather x1, waiting for transfers between devices, on_device(): roots = lax.all_gather(own_rows, 'lev', axis=2, tiled=True)  20 us
    unnamed x38, local copies, waits for them, and re-layouts  8.58 us
    dot_general x2, matrix products, on_device(): observed = jnp.einsum('tcj,jto->tco', all_jacs, picked, precision=highest)  6.51 us
    dot_general x2, matrix products, on_device(): jnp.dot(jnp.concatenate([high, low], axis=0), column_marks, preferred_ele...  4.84 us
  transfers between devices with their start and end apart: 4, of which 2 were waited for; matrix products, arithmetic and copies ran while one was open for 12% of the time, Pallas kernels for 23%

profile of v1, /device:TPU:0, one launch (start us, length us, event | category | flops | bytes accessed | tf_op | source)
XLA Modules:
  0.0 236.9 jit_solution(12670934341873882072)
XLA Ops:
  7.3 1.7 copy.97
  13.2 1.7 fusion.8
  15.1 29.8 %exchange.1 = (f32[8,2,32,128]{3,2,1,0:T(8,128)S(1)}, f32[8,128,64]{2,1,0:T(8,128)S(1)}, f32[8,2,8,128]{3,2,1,0:T(8,128)S(1)}, f32[8,72,256]{2,1,0:T(8,128)S(1)}) custom-call(f32[2,32,128]{2,1,0:T(8,128)S(1)} %bitcast.139, f32[128,64]{1,0:T(8,128)S(1)} %copy.93.jacobian, f32[2,8,128]{2,1,0:T(8,128)S(1)} %multiply_reduce_fusion.kappa, f32[8,72,256]{2,1,0:T(8,128)S(1)} %bitcast.126), custom_call_target="tpu_custom_call" | custom-call | tf_op jit(solution)/shard_map/exchange/pallas_call | solution.py:308
  48.9 1.6 copy.98
  51.9 20.0 %all-gather.11.cloned.1.call-done = f32[8,2,128,128]{3,2,1,0:T(8,128)} async-done(((f32[8,2,32,128]{3,2,1,0:T(8,128)}), f32[8,2,128,128]{3,2,1,0:T(8,128)}) %all-gather.11.cloned.1.call-update) | async-done | bytes 1048592 | tf_op jit(solution)/shard_map/all_gather | solution.py:425
  71.9 2.3 fusion.67
  74.6 1.3 maximum_bitcast_fusion
  75.9 1.5 copy.114
  77.5 24.2 %forward.3 = f32[4,2,8,32,128]{4,3,2,1,0:T(8,128)S(1)} custom-call(f32[2,8,32,128]{3,2,1,0:T(8,128)S(1)} %bitcast.129, f32[2,8,32,128]{3,2,1,0:T(8,128)S(1)} %bitcast.127, f32[2,2,8,32,128]{4,3,2,1,0:T(8,128)S(1)} %convert_bitcast_fusion.perts, f32[2,5,16,8,128]{4,3,2,1,0:T(8,128)S(1)} %broadcast_in_dim.39.w_ref), custom_call_target="tpu_custom_call" | custom-call | tf_op jit(solution)/shard_map/forward/pallas_call | solution.py:308
  102.6 2.4 %fusion.3 = f32[512,2048]{1,0:T(8,128)S(1)} fusion(s32[2048]{0:T(1024)S(1)} %bitcast.161, bf16[256,1024]{1,0:T(8,128)(2,1)S(1)} %get-tuple-element.44, bf16[256,1024]{1,0:T(8,128)(2,1)S(1)} %get-tuple-element.43), kind=kOutput, calls=%fused_computation.5 | convolution fusion | flops 2151677952 | bytes 5251072 | tf_op jit(solution)/shard_map/dot_general | solution.py:460
  105.1 1.6 slice_add_fusion.1
  106.7 2.5 %copy.137 = f32[32,8,8,256]{3,2,1,0:T(8,128)S(1)} copy(f32[32,8,8,256]{3,1,2,0:T(8,128)} %bitcast.151) | data formatting | bytes 4194304
  111.9 3.4 %all-gather.7.cloned.1.call-done = f32[8,128,256]{1,0,2:T(8,128)} async-done(((f32[8,128,64]{1,0,2:T(8,128)}), f32[8,128,256]{1,0,2:T(8,128)}) %all-gather.7.cloned.1.call-update) | async-done | bytes 1048592 | tf_op jit(solution)/shard_map/all_gather | solution.py:422
  115.3 4.5 %fusion.25 = f32[8,128,256]{2,1,0:T(8,128)S(1)} fusion(f32[8,128,256]{2,1,0:T(8,128)} %bitcast.142, f32[8,128,256]{2,1,0:T(8,128)} %bitcast.140, f32[32,8,8,256]{3,2,1,0:T(8,128)} %bitcast.144, f32[8,128,256]{1,0,2:T(8,128)} %all-gather.7.cloned.1.call-done), kind=kOutput, calls=%fused_computation.29 | convolution fusion | flops 805830656 | bytes 6291456 | tf_op jit(solution)/shard_map/tcj,jto->tco/dot_general | solution.py:463
  121.1 1.9 fusion.2
  123.2 19.1 %backward.2 = (f32[4,2,8,32,128]{4,3,2,1,0:T(8,128)S(1)}, f32[2,8,32,128]{3,2,1,0:T(8,128)S(1)}) custom-call(f32[2,8,32,128]{3,2,1,0:T(8,128)S(1)} %bitcast.133, f32[2,8,32,128]{3,2,1,0:T(8,128)S(1)} %bitcast.128, f32[2,2,8,32,128]{4,3,2,1,0:T(8,128)S(1)} %convert_bitcast_fusion.perts, f32[2,5,16,8,128]{4,3,2,1,0:T(8,128)S(1)} %broadcast_in_dim.39.w_ref), custom_call_target="tpu_custom_call" | custom-call | tf_op jit(solution)/shard_map/backward/pallas_call | solution.py:308
  142.3 4.9 %vertical.2 = (f32[2,8,32,128]{3,2,1,0:T(8,128)S(1)}, f32[2,8,32,128]{3,2,1,0:T(8,128)S(1)}) custom-call(f32[4,2,8,32,128]{4,3,2,1,0:T(8,128)S(1)} %get-tuple-element.19.full, f32[2,512,128]{2,1,0:T(8,128)S(1)} %bitcast.122, f32[2,8,32,128]{3,2,1,0:T(8,128)S(1)} %bitcast.135, f32[2,8,32,128]{3,2,1,0:T(8,128)S(1)} %bitcast.130), custom_call_target="tpu_custom_call" | custom-call | tf_op jit(solution)/shard_map/vertical/pallas_call | solution.py:308
  147.2 26.7 %forward.4 = f32[4,2,8,32,128]{4,3,2,1,0:T(8,128)S(1)} custom-call(f32[2,8,32,128]{3,2,1,0:T(8,128)S(1)} %get-tuple-element.20.mixed, f32[2,8,32,128]{3,2,1,0:T(8,128)S(1)} %get-tuple-element.21.ensemble, f32[2,2,8,32,128]{4,3,2,1,0:T(8,128)S(1)} %convert_bitcast_fusion.perts, f32[2,5,16,8,128]{4,3,2,1,0:T(8,128)S(1)} %broadcast_in_dim.39.w_ref), custom_call_target="tpu_custom_call" | custom-call | tf_op jit(solution)/shard_map/forward/pallas_call | solution.py:308
  174.9 2.4 %fusion.1 = f32[512,2048]{1,0:T(8,128)S(1)} fusion(s32[2048]{0:T(1024)S(1)} %bitcast.163, bf16[256,1024]{1,0:T(8,128)(2,1)S(1)} %get-tuple-element.42, bf16[256,1024]{1,0:T(8,128)(2,1)S(1)} %get-tuple-element.41), kind=kOutput, calls=%fused_computation.3 | convolution fusion | flops 2151677952 | bytes 5251072 | tf_op jit(solution)/shard_map/dot_general | solution.py:460
  179.1 2.0 fusion.22
  182.5 1.9 fusion
  184.6 20.7 %backward.3 = (f32[4,2,8,32,128]{4,3,2,1,0:T(8,128)S(1)}, f32[2,8,32,128]{3,2,1,0:T(8,128)S(1)}) custom-call(f32[2,8,32,128]{3,2,1,0:T(8,128)S(1)} %bitcast.134, f32[2,8,32,128]{3,2,1,0:T(8,128)S(1)} %get-tuple-element.21.ensemble, f32[2,2,8,32,128]{4,3,2,1,0:T(8,128)S(1)} %convert_bitcast_fusion.perts, f32[2,5,16,8,128]{4,3,2,1,0:T(8,128)S(1)} %broadcast_in_dim.39.w_ref), custom_call_target="tpu_custom_call" | custom-call | tf_op jit(solution)/shard_map/backward/pallas_call | solution.py:308
  205.3 4.7 %vertical.3 = (f32[2,8,32,128]{3,2,1,0:T(8,128)S(1)}, f32[2,8,32,128]{3,2,1,0:T(8,128)S(1)}) custom-call(f32[4,2,8,32,128]{4,3,2,1,0:T(8,128)S(1)} %get-tuple-element.22.full, f32[2,512,128]{2,1,0:T(8,128)S(1)} %bitcast.123, f32[2,8,32,128]{3,2,1,0:T(8,128)S(1)} %get-tuple-element.23.static, f32[2,8,32,128]{3,2,1,0:T(8,128)S(1)} %get-tuple-element.20.mixed), custom_call_target="tpu_custom_call" | custom-call | tf_op jit(solution)/shard_map/vertical/pallas_call | solution.py:308
  210.0 17.8 %forward.5 = f32[2,8,32,128]{3,2,1,0:T(8,128)S(1)} custom-call(f32[2,8,32,128]{3,2,1,0:T(8,128)S(1)} %get-tuple-element.24.mixed, f32[2,8,32,128]{3,2,1,0:T(8,128)S(1)} %get-tuple-element.25.ensemble, f32[2,2,8,32,128]{4,3,2,1,0:T(8,128)S(1)} %convert_bitcast_fusion.perts, f32[2,5,16,8,128]{4,3,2,1,0:T(8,128)S(1)} %broadcast_in_dim.39.w_ref), custom_call_target="tpu_custom_call" | custom-call | tf_op jit(solution)/shard_map/forward/pallas_call | solution.py:308
  (97 shorter events, 21.8 us)
Async XLA Ops:
  7.2 7.8 %copy-start.10 = (f32[8]{0:T(128)S(1)}, f32[8]{0:T(128)}, u32[]{:S(2)}) copy-start(f32[8]{0:T(128)} %param.20) | copy-start | bytes 100
  7.2 7.8 %copy-start.11 = (f32[8]{0:T(128)S(1)}, f32[8]{0:T(128)}, u32[]{:S(2)}) copy-start(f32[8]{0:T(128)} %param.19) | copy-start | bytes 100
  7.2 7.8 %copy-start.9 = (s32[8,128]{1,0:T(8,128)S(1)}, s32[8,128]{1,0:T(8,128)}, u32[]{:S(2)}) copy-start(s32[8,128]{1,0:T(8,128)} %param.18) | copy-start | bytes 12292
  7.2 7.9 %copy-start = (f32[1,2,32,128]{3,2,1,0:T(8,128)S(1)}, f32[1,2,32,128]{3,2,1,0:T(8,128)}, u32[]{:S(2)}) copy-start(f32[1,2,32,128]{3,2,1,0:T(8,128)} %param.16) | copy-start | bytes 98308
  7.2 41.7 %all-gather.9.cloned.1.call-start = ((), (), s32[]{:S(2)}) async-start(), calls=%async_computation.2 | async-start | bytes 1310720 | tf_op jit(solution)/shard_map/all_gather | solution.py:454
  8.9 63.0 %all-gather.11.cloned.1.call-start = ((), (), s32[]{:S(2)}) async-start(), calls=%async_computation.3 | async-start | bytes 1310720 | tf_op jit(solution)/shard_map/all_gather | solution.py:425
  9.7 35.2 %copy-start.12 = (s32[8]{0:T(128)S(1)}, s32[8]{0:T(128)}, u32[]{:S(2)}) copy-start(s32[8]{0:T(128)} %param.17) | copy-start | bytes 100
  46.3 2.0 copy-start.6
  46.3 60.4 %all-gather.5.cloned.1.call-start = ((), (), s32[]{:S(2)}) async-start(), calls=%async_computation | async-start | bytes 2621440 | tf_op jit(solution)/shard_map/all_gather | solution.py:417
  46.4 2.2 copy-start.8
  46.4 2.2 copy-start.7
  47.3 68.0 %all-gather.7.cloned.1.call-start = ((), (), s32[]{:S(2)}) async-start(), calls=%async_computation.1 | async-start | bytes 1310720 | tf_op jit(solution)/shard_map/all_gather | solution.py:422
  51.5 20.4 %copy-start.5 = (f32[8,2,32,128]{3,2,1,0:T(8,128)S(1)}, f32[8,2,32,128]{3,2,1,0:T(8,128)}, u32[]{:S(2)}) copy-start(f32[8,2,32,128]{3,2,1,0:T(8,128)} %broadcast_select_fusion) | copy-start | bytes 786436
  71.9 2.3 copy-start.3
  177.3 1.2 copy-start.1
  177.3 1.5 copy-start.2
  177.3 1.8 copy-start.4
Sparse Core Ops, SparseCore 0:
  10.2 19.4 all-gather.8
  46.4 25.4 all-gather.10
  73.5 22.5 all-gather.4
  98.1 17.1 all-gather.6

commit v2 on v1

--- a/solution.py
+++ b/solution.py
@@ -133,11 +133,13 @@
     copies += [
         halo_copies(ensemble.at[e], halo, variables + e, hsend, hrecv) for e in range(members)
     ]
-    for pair in copies:
-        for copy in pair:
+    order = [variables + e for e in range(members)] + list(range(variables))
+    for field in order:
+        for copy in copies[field]:
             copy.start()
     block = out.at[me] if spread else out
-    for field in range(variables + members):
+    plans = [spread_copies(out, v, lsend, lrecv) for v in range(variables)] if spread else []
+    for field in order:
         for copy in copies[field]:
             copy.wait_recv()
         static = field < variables
@@ -147,26 +149,27 @@
         def body(rows):
             result = forward_rows(widened(own, halo, field, rows), weights)
             if static:
-                block[field, :, rows] = beta_static * result
+                block[field, :, rows] += beta_static * result
             else:
                 result = beta_ensemble * result
                 for v in range(variables):
-                    block[v, :, rows] += perts[field - variables, v, :, rows] * result
+                    term = perts[field - variables, v, :, rows] * result
+                    if field > variables:
+                        term = block[v, :, rows] + term
+                    block[v, :, rows] = term
 
         over_rows(levels, body)
+        if static and spread:
+            plans[field][1].start()
+            plans[field][0].start()
     if spread:
-        plans = [spread_copies(out, v, lsend, lrecv) for v in range(variables)]
-        finish_spread(plans, start=True)
+        finish_spread(plans)
     for pair in copies:
         for copy in pair:
             copy.wait_send()
 
 
-def finish_spread(plans, start):
-    if start:
-        for plan in plans:
-            plan[1].start()
-            plan[0].start()
+def finish_spread(plans):
     for plan in plans:
         plan[1].wait_recv()
         plan[2].start()
@@ -221,7 +224,7 @@
         if static:
             plans[field][1].start()
             plans[field][0].start()
-    finish_spread(plans, start=False)
+    finish_spread(plans)
     for pair in copies:
         for copy in pair:
             copy.wait_send()
@@ -423,10 +426,6 @@
 
     own_rows = jnp.take(own_rows, band_owner, axis=0)
     roots = lax.all_gather(own_rows, "lev", axis=2, tiled=True)
-    own_columns = lax.dynamic_slice_in_dim(roots, lev_index * levels, levels, axis=3)
-    squares = jnp.einsum("bvlm,bvkm->bvlk", own_rows, roots, precision=highest)
-    update = jnp.concatenate([own_columns.transpose(0, 1, 3, 2), squares], axis=2)
-    update = update.transpose(1, 0, 2, 3).reshape(variables, -1, all_levels)
 
     def vertical(matrices, full):
         shaped = full.reshape(variables, all_levels, lons, bands, height)
@@ -475,6 +474,12 @@
             backward_kernel, "backward", 3, [shape(levs, *block), shape(members, *block[1:])],
             [source, halo] + halo_sems + lev_sems, gradient, ensemble, perts, wide_weights,
         )
+        if iteration == 0:
+            roots, full = lax.optimization_barrier((roots, full))
+            own_columns = lax.dynamic_slice_in_dim(roots, lev_index * levels, levels, axis=3)
+            squares = jnp.einsum("bvlm,bvkm->bvlk", own_rows, roots, precision=highest)
+            update = jnp.concatenate([own_columns.transpose(0, 1, 3, 2), squares], axis=2)
+            update = update.transpose(1, 0, 2, 3).reshape(variables, -1, all_levels)
         static, mixed = call(
             vertical_kernel, "vertical", None, [shape(*block), shape(*block)], [],
             full, update, static, mixed,

time: 237 us -> 226 us (0.954)
  waiting for transfers between devices: 23.5 us -> 6.4 us
  Pallas kernels: 148 us -> 152 us
    all_gather x1, waiting for transfers between devices: 20 us -> 0.01 us  [on_device(): roots = lax.all_gather(own_rows, 'lev', axis=2, tiled=True)]
    pallas_call x8, Pallas kernels: 148 us -> 152 us  [call(): pl.pallas_call(kernel, name=name, out_shape=shapes if many else [shapes],...]
    all_gather x1, waiting for transfers between devices: 3.43 us -> 6.31 us  [on_device(): all_jacs = lax.all_gather(jacs, 'lev', axis=2, tiled=True)]
    unnamed x38 -> x46, local copies, waits for them, and re-layouts: 8.58 us -> 11 us
  transfers between devices with their start and end apart: 4 -> 4, of which waited for: 2 -> 1; matrix products, arithmetic and copies ran while one was open for 12% -> 13% of each run, Pallas kernels for 23% -> 35%
where the time goes in v2:
time: 226 us; the launch traced here: 225 us
  Pallas kernels  152 us (67%)
  matrix products  22.9 us (10%)
  local copies, waits for them, and re-layouts  22.8 us (10%)
  between operations  14.4 us (6%)
  other arithmetic  6.57 us (3%)
  waiting for transfers between devices  6.4 us (3%)
    pallas_call x8, Pallas kernels, call(): pl.pallas_call(kernel, name=name, out_shape=shapes if many else [shapes],...  152 us
    unnamed x46, local copies, waits for them, and re-layouts  11 us
    all_gather x1, waiting for transfers between devices, on_device(): all_jacs = lax.all_gather(jacs, 'lev', axis=2, tiled=True)  6.31 us
    dot_general x2, matrix products, on_device(): observed = jnp.einsum('tcj,jto->tco', all_jacs, picked, precision=highest)  6.2 us
    dot_general x2, matrix products, on_device(): jnp.dot(jnp.concatenate([high, low], axis=0), column_marks, preferred_ele...  4.84 us
  transfers between devices with their start and end apart: 4, of which 1 were waited for; matrix products, arithmetic and copies ran while one was open for 13% of the time, Pallas kernels for 35%

profile of v2, /device:TPU:0, one launch (start us, length us, event | category | flops | bytes accessed | tf_op | source)
XLA Modules:
  0.0 225.3 jit_solution(12633786170696832043)
XLA Ops:
  7.3 1.7 copy.97
  12.3 1.7 fusion.8
  14.4 29.8 %exchange.1 = (f32[8,2,32,128]{3,2,1,0:T(8,128)S(1)}, f32[8,128,64]{2,1,0:T(8,128)S(1)}, f32[8,2,8,128]{3,2,1,0:T(8,128)S(1)}, f32[8,72,256]{2,1,0:T(8,128)S(1)}) custom-call(f32[2,32,128]{2,1,0:T(8,128)S(1)} %bitcast.139, f32[128,64]{1,0:T(8,128)S(1)} %copy.93.jacobian, f32[2,8,128]{2,1,0:T(8,128)S(1)} %multiply_reduce_fusion.kappa, f32[8,72,256]{2,1,0:T(8,128)S(1)} %bitcast.126), custom_call_target="tpu_custom_call" | custom-call | tf_op jit(solution)/shard_map/exchange/pallas_call | solution.py:311
  48.8 1.6 copy.98
  51.9 30.0 %forward.3 = f32[4,2,8,32,128]{4,3,2,1,0:T(8,128)S(1)} custom-call(f32[2,8,32,128]{3,2,1,0:T(8,128)S(1)} %bitcast.129, f32[2,8,32,128]{3,2,1,0:T(8,128)S(1)} %bitcast.127, f32[2,2,8,32,128]{4,3,2,1,0:T(8,128)S(1)} %convert_bitcast_fusion.perts, f32[2,5,16,8,128]{4,3,2,1,0:T(8,128)S(1)} %broadcast_in_dim.39.w_ref), custom_call_target="tpu_custom_call" | custom-call | tf_op jit(solution)/shard_map/forward/pallas_call | solution.py:311
  82.8 2.4 %fusion.3 = f32[512,2048]{1,0:T(8,128)S(1)} fusion(s32[2048]{0:T(1024)S(1)} %bitcast.161, bf16[256,1024]{1,0:T(8,128)(2,1)S(1)} %get-tuple-element.48, bf16[256,1024]{1,0:T(8,128)(2,1)S(1)} %get-tuple-element.47), kind=kOutput, calls=%fused_computation.5 | convolution fusion | flops 2151677952 | bytes 5251072 | tf_op jit(solution)/shard_map/dot_general | solution.py:459
  85.2 1.6 slice_add_fusion.1
  86.9 2.5 %copy.137 = f32[32,8,8,256]{3,2,1,0:T(8,128)S(1)} copy(f32[32,8,8,256]{3,1,2,0:T(8,128)} %bitcast.151) | data formatting | bytes 4194304
  89.9 1.3 copy.109
  91.2 6.3 %all-gather.7.cloned.1.call-done = f32[8,128,256]{1,0,2:T(8,128)} async-done(((f32[8,128,64]{1,0,2:T(8,128)}), f32[8,128,256]{1,0,2:T(8,128)}) %all-gather.7.cloned.1.call-update) | async-done | bytes 1048592 | tf_op jit(solution)/shard_map/all_gather | solution.py:425
  97.5 4.2 %fusion.25 = f32[8,128,256]{2,1,0:T(8,128)S(1)} fusion(f32[8,128,256]{2,1,0:T(8,128)S(1)} %bitcast.140, f32[8,128,256]{2,1,0:T(8,128)} %bitcast.142, f32[32,8,8,256]{3,2,1,0:T(8,128)} %bitcast.144, f32[8,128,256]{1,0,2:T(8,128)} %all-gather.7.cloned.1.call-done), kind=kOutput, calls=%fused_computation.29 | convolution fusion | flops 805830656 | bytes 6291456 | tf_op jit(solution)/shard_map/tcj,jto->tco/dot_general | solution.py:462
  103.0 1.9 fusion.2
  105.1 19.1 %backward.2 = (f32[4,2,8,32,128]{4,3,2,1,0:T(8,128)S(1)}, f32[2,8,32,128]{3,2,1,0:T(8,128)S(1)}) custom-call(f32[2,8,32,128]{3,2,1,0:T(8,128)S(1)} %bitcast.133, f32[2,8,32,128]{3,2,1,0:T(8,128)S(1)} %bitcast.128, f32[2,2,8,32,128]{4,3,2,1,0:T(8,128)S(1)} %convert_bitcast_fusion.perts, f32[2,5,16,8,128]{4,3,2,1,0:T(8,128)S(1)} %broadcast_in_dim.39.w_ref), custom_call_target="tpu_custom_call" | custom-call | tf_op jit(solution)/shard_map/backward/pallas_call | solution.py:311
  124.9 1.6 dynamic-slice_bitcast_fusion
  126.6 1.9 fusion.67
  129.9 1.5 copy.114
  132.4 4.7 %vertical.2 = (f32[2,8,32,128]{3,2,1,0:T(8,128)S(1)}, f32[2,8,32,128]{3,2,1,0:T(8,128)S(1)}) custom-call(f32[4,2,8,32,128]{4,3,2,1,0:T(8,128)S(1)} %get-tuple-element.22.full, f32[2,512,128]{2,1,0:T(8,128)S(1)} %bitcast.122, f32[2,8,32,128]{3,2,1,0:T(8,128)S(1)} %bitcast.135, f32[2,8,32,128]{3,2,1,0:T(8,128)S(1)} %bitcast.130), custom_call_target="tpu_custom_call" | custom-call | tf_op jit(solution)/shard_map/vertical/pallas_call | solution.py:311
  137.1 25.3 %forward.4 = f32[4,2,8,32,128]{4,3,2,1,0:T(8,128)S(1)} custom-call(f32[2,8,32,128]{3,2,1,0:T(8,128)S(1)} %get-tuple-element.24.mixed, f32[2,8,32,128]{3,2,1,0:T(8,128)S(1)} %copy-done.2, f32[2,2,8,32,128]{4,3,2,1,0:T(8,128)S(1)} %convert_bitcast_fusion.perts, f32[2,5,16,8,128]{4,3,2,1,0:T(8,128)S(1)} %broadcast_in_dim.39.w_ref), custom_call_target="tpu_custom_call" | custom-call | tf_op jit(solution)/shard_map/forward/pallas_call | solution.py:311
  163.3 2.4 %fusion.1 = f32[512,2048]{1,0:T(8,128)S(1)} fusion(s32[2048]{0:T(1024)S(1)} %bitcast.163, bf16[256,1024]{1,0:T(8,128)(2,1)S(1)} %get-tuple-element.46, bf16[256,1024]{1,0:T(8,128)(2,1)S(1)} %get-tuple-element.45), kind=kOutput, calls=%fused_computation.3 | convolution fusion | flops 2151677952 | bytes 5251072 | tf_op jit(solution)/shard_map/dot_general | solution.py:459
  167.6 2.0 fusion.22
  170.9 1.9 fusion
  173.0 20.7 %backward.3 = (f32[4,2,8,32,128]{4,3,2,1,0:T(8,128)S(1)}, f32[2,8,32,128]{3,2,1,0:T(8,128)S(1)}) custom-call(f32[2,8,32,128]{3,2,1,0:T(8,128)S(1)} %bitcast.134, f32[2,8,32,128]{3,2,1,0:T(8,128)S(1)} %copy-done.2, f32[2,2,8,32,128]{4,3,2,1,0:T(8,128)S(1)} %convert_bitcast_fusion.perts, f32[2,5,16,8,128]{4,3,2,1,0:T(8,128)S(1)} %broadcast_in_dim.39.w_ref), custom_call_target="tpu_custom_call" | custom-call | tf_op jit(solution)/shard_map/backward/pallas_call | solution.py:311
  193.7 4.7 %vertical.3 = (f32[2,8,32,128]{3,2,1,0:T(8,128)S(1)}, f32[2,8,32,128]{3,2,1,0:T(8,128)S(1)}) custom-call(f32[4,2,8,32,128]{4,3,2,1,0:T(8,128)S(1)} %get-tuple-element.26.full, f32[2,512,128]{2,1,0:T(8,128)S(1)} %bitcast.123, f32[2,8,32,128]{3,2,1,0:T(8,128)S(1)} %get-tuple-element.27.static, f32[2,8,32,128]{3,2,1,0:T(8,128)S(1)} %get-tuple-element.24.mixed), custom_call_target="tpu_custom_call" | custom-call | tf_op jit(solution)/shard_map/vertical/pallas_call | solution.py:311
  198.4 17.7 %forward.5 = f32[2,8,32,128]{3,2,1,0:T(8,128)S(1)} custom-call(f32[2,8,32,128]{3,2,1,0:T(8,128)S(1)} %get-tuple-element.28.mixed, f32[2,8,32,128]{3,2,1,0:T(8,128)S(1)} %get-tuple-element.29.ensemble, f32[2,2,8,32,128]{4,3,2,1,0:T(8,128)S(1)} %convert_bitcast_fusion.perts, f32[2,5,16,8,128]{4,3,2,1,0:T(8,128)S(1)} %broadcast_in_dim.39.w_ref), custom_call_target="tpu_custom_call" | custom-call | tf_op jit(solution)/shard_map/forward/pallas_call | solution.py:311
  (105 shorter events, 22.1 us)
Async XLA Ops:
  7.2 6.9 %copy-start.12 = (f32[1,128,2,32]{1,3,2,0:T(8,128)S(1)}, f32[1,128,2,32]{1,3,2,0:T(8,128)}, u32[]{:S(2)}) copy-start(f32[1,128,2,32]{1,3,2,0:T(8,128)} %param.23) | copy-start | bytes 98308
  7.2 7.0 %copy-start.15 = (f32[8]{0:T(128)S(1)}, f32[8]{0:T(128)}, u32[]{:S(2)}) copy-start(f32[8]{0:T(128)} %param.19) | copy-start | bytes 100
  7.2 7.0 %copy-start.14 = (f32[8]{0:T(128)S(1)}, f32[8]{0:T(128)}, u32[]{:S(2)}) copy-start(f32[8]{0:T(128)} %param.20) | copy-start | bytes 100
  7.2 7.0 %copy-start.13 = (s32[8,128]{1,0:T(8,128)S(1)}, s32[8,128]{1,0:T(8,128)}, u32[]{:S(2)}) copy-start(s32[8,128]{1,0:T(8,128)} %param.18) | copy-start | bytes 12292
  7.2 7.1 %copy-start.3 = (f32[1,2,32,128]{3,2,1,0:T(8,128)S(1)}, f32[1,2,32,128]{3,2,1,0:T(8,128)}, u32[]{:S(2)}) copy-start(f32[1,2,32,128]{3,2,1,0:T(8,128)} %param.16) | copy-start | bytes 98308
  7.2 41.6 %all-gather.11.cloned.1.call-start = ((), (), s32[]{:S(2)}) async-start(), calls=%async_computation.3 | async-start | bytes 1310720 | tf_op jit(solution)/shard_map/all_gather | solution.py:453
  9.0 77.9 %all-gather.5.cloned.1.call-start = ((), (), s32[]{:S(2)}) async-start(), calls=%async_computation | async-start | bytes 2621440 | tf_op jit(solution)/shard_map/all_gather | solution.py:420
  14.4 31.7 %copy-start.16 = (s32[8]{0:T(128)S(1)}, s32[8]{0:T(128)}, u32[]{:S(2)}) copy-start(s32[8]{0:T(128)} %param.17) | copy-start | bytes 100
  44.2 3.5 %copy-start.9 = (f32[2,32,8,128]{3,2,1,0:T(8,128)S(1)}, f32[2,32,8,128]{3,2,1,0:T(8,128)}, u32[]{:S(2)}) copy-start(f32[2,32,8,128]{3,2,1,0:T(8,128)} %param.13) | copy-start | bytes 786436
  45.0 3.6 %copy-start.10 = (bf16[2,2,32,8,128]{4,3,2,1,0:T(8,128)(2,1)S(1)}, bf16[2,2,32,8,128]{4,3,2,1,0:T(8,128)(2,1)}, u32[]{:S(2)}) copy-start(bf16[2,2,32,8,128]{4,3,2,1,0:T(8,128)(2,1)} %param.15) | copy-start | bytes 786436
  45.1 52.5 %all-gather.7.cloned.1.call-start = ((), (), s32[]{:S(2)}) async-start(), calls=%async_computation.1 | async-start | bytes 1310720 | tf_op jit(solution)/shard_map/all_gather | solution.py:425
  45.1 3.6 %copy-start.11 = (f32[2,32,8,128]{3,2,1,0:T(8,128)S(1)}, f32[2,32,8,128]{3,2,1,0:T(8,128)}, u32[]{:S(2)}) copy-start(f32[2,32,8,128]{3,2,1,0:T(8,128)} %param.14) | copy-start | bytes 786436
  46.0 78.9 %all-gather.9.cloned.1.call-start = ((), (), s32[]{:S(2)}) async-start(), calls=%async_computation.2 | async-start | bytes 1310720 | tf_op jit(solution)/shard_map/all_gather | solution.py:428
  89.9 11.8 %copy-start.4 = (f32[1,8,4,32,256]{4,3,2,1,0:T(8,128)}, f32[1,8,4,32,256]{4,3,2,1,0:T(8,128)S(1)}, u32[]{:S(2)}) copy-start(f32[1,8,4,32,256]{4,3,2,1,0:T(8,128)S(1)} %copy.95) | copy-start | bytes 3145732
  124.2 0.7 copy-start.1
  124.9 1.7 copy-start.7
  131.4 1.0 copy-start
  132.4 4.7 %copy-start.2 = (f32[2,8,32,128]{3,2,1,0:T(8,128)S(1)}, f32[2,8,32,128]{3,2,1,0:T(8,128)}, u32[]{:S(2)}) copy-start(f32[2,8,32,128]{3,2,1,0:T(8,128)} %copy-done.1) | copy-start | bytes 786436
  165.7 1.2 copy-start.5
  165.7 1.5 copy-start.6
  165.7 1.8 copy-start.8
Sparse Core Ops, SparseCore 0:
  10.2 19.4 all-gather.10
  45.2 32.5 all-gather.4
  79.9 17.5 all-gather.6
  99.5 16.7 all-gather.8

commit v3 on v2

--- a/solution.py
+++ b/solution.py
@@ -459,9 +459,9 @@
         picked = jnp.dot(jnp.concatenate([high, low], axis=0), column_marks,
                          preferred_element_type=jnp.float32)
         picked = (picked[:full.shape[0]] + picked[full.shape[0]:]).reshape(-1, tiles, capacity)
-        observed = jnp.einsum("tcj,jto->tco", all_jacs, picked, precision=highest)
+        observed = jnp.einsum("tcj,jto->tco", all_jacs, picked, precision=lax.Precision.HIGH)
         weighted = slot_weight * (observed - slot_innovation)
-        pulled = jnp.einsum("tcj,tco->jto", jacs, weighted, precision=highest)
+        pulled = jnp.einsum("tcj,tco->jto", jacs, weighted, precision=lax.Precision.HIGH)
         pulled = pulled.reshape(-1, slots)
         high, low = split2(pulled)
         gradient = lax.dot_general(

time: 226 us -> 223 us (0.987)
  matrix products: 22.9 us -> 20.3 us
    dot_general x4, matrix products: 8.57 us -> 6 us  [the longest x2 4.64 us: on_device(): jnp.einsum('tcj,jto->tco', all_jacs, picked, precision=lax.Precision.HIGH)]
where the time goes in v3:
time: 223 us
  Pallas kernels  152 us (68%)
  local copies, waits for them, and re-layouts  22.8 us (10%)
  matrix products  20.3 us (9%)
  between operations  14.4 us (6%)
  other arithmetic  6.57 us (3%)
  waiting for transfers between devices  6.4 us (3%)
    pallas_call x8, Pallas kernels, call(): pl.pallas_call(kernel, name=name, out_shape=shapes if many else [shapes],...  152 us
    unnamed x46, local copies, waits for them, and re-layouts  11 us
    all_gather x1, waiting for transfers between devices, on_device(): all_jacs = lax.all_gather(jacs, 'lev', axis=2, tiled=True)  6.31 us
    dot_general x2, matrix products, on_device(): jnp.dot(jnp.concatenate([high, low], axis=0), column_marks, preferred_ele...  4.84 us
    dot_general x2, matrix products, on_device(): jnp.einsum('tcj,jto->tco', all_jacs, picked, precision=lax.Precision.HIGH)  4.64 us
  transfers between devices with their start and end apart: 4, of which 1 were waited for; matrix products, arithmetic and copies ran while one was open for 13% of the time, Pallas kernels for 35%

profile of v3, /device:TPU:0, one launch (start us, length us, event | category | flops | bytes accessed | tf_op | source)
XLA Modules:
  0.0 222.9 jit_solution(12248237028017104490)
XLA Ops:
  7.3 1.7 copy.97
  12.3 1.7 fusion.8
  14.4 29.8 %exchange.1 = (f32[8,2,32,128]{3,2,1,0:T(8,128)S(1)}, f32[8,128,64]{2,1,0:T(8,128)S(1)}, f32[8,2,8,128]{3,2,1,0:T(8,128)S(1)}, f32[8,72,256]{2,1,0:T(8,128)S(1)}) custom-call(f32[2,32,128]{2,1,0:T(8,128)S(1)} %bitcast.139, f32[128,64]{1,0:T(8,128)S(1)} %copy.93.jacobian, f32[2,8,128]{2,1,0:T(8,128)S(1)} %multiply_reduce_fusion.kappa, f32[8,72,256]{2,1,0:T(8,128)S(1)} %bitcast.126), custom_call_target="tpu_custom_call" | custom-call | tf_op jit(solution)/shard_map/exchange/pallas_call | solution.py:311
  48.8 1.6 copy.98
  51.9 30.0 %forward.3 = f32[4,2,8,32,128]{4,3,2,1,0:T(8,128)S(1)} custom-call(f32[2,8,32,128]{3,2,1,0:T(8,128)S(1)} %bitcast.129, f32[2,8,32,128]{3,2,1,0:T(8,128)S(1)} %bitcast.127, f32[2,2,8,32,128]{4,3,2,1,0:T(8,128)S(1)} %convert_bitcast_fusion.perts, f32[2,5,16,8,128]{4,3,2,1,0:T(8,128)S(1)} %broadcast_in_dim.39.w_ref), custom_call_target="tpu_custom_call" | custom-call | tf_op jit(solution)/shard_map/forward/pallas_call | solution.py:311
  82.8 2.4 %fusion.3 = f32[512,2048]{1,0:T(8,128)S(1)} fusion(s32[2048]{0:T(1024)S(1)} %bitcast.161, bf16[256,1024]{1,0:T(8,128)(2,1)S(1)} %get-tuple-element.48, bf16[256,1024]{1,0:T(8,128)(2,1)S(1)} %get-tuple-element.47), kind=kOutput, calls=%fused_computation.5 | convolution fusion | flops 2151677952 | bytes 5251072 | tf_op jit(solution)/shard_map/dot_general | solution.py:459
  85.2 1.6 slice_add_fusion.1
  86.9 2.5 %copy.137 = f32[32,8,8,256]{3,2,1,0:T(8,128)S(1)} copy(f32[32,8,8,256]{3,1,2,0:T(8,128)} %bitcast.151) | data formatting | bytes 4194304
  89.9 1.3 copy.109
  91.2 6.3 %all-gather.7.cloned.1.call-done = f32[8,128,256]{1,0,2:T(8,128)} async-done(((f32[8,128,64]{1,0,2:T(8,128)}), f32[8,128,256]{1,0,2:T(8,128)}) %all-gather.7.cloned.1.call-update) | async-done | bytes 1048592 | tf_op jit(solution)/shard_map/all_gather | solution.py:425
  97.5 3.4 %fusion.25 = f32[8,128,256]{2,1,0:T(8,128)S(1)} fusion(f32[8,128,256]{2,1,0:T(8,128)S(1)} %bitcast.140, f32[8,128,256]{2,1,0:T(8,128)} %bitcast.142, f32[32,8,8,256]{3,2,1,0:T(8,128)} %bitcast.144, f32[8,128,256]{1,0,2:T(8,128)} %all-gather.7.cloned.1.call-done), kind=kOutput, calls=%fused_computation.29 | convolution fusion | flops 403177472 | bytes 6291456 | tf_op jit(solution)/shard_map/tcj,jto->tco/dot_general | solution.py:462
  101.7 1.9 fusion.2
  103.8 19.1 %backward.2 = (f32[4,2,8,32,128]{4,3,2,1,0:T(8,128)S(1)}, f32[2,8,32,128]{3,2,1,0:T(8,128)S(1)}) custom-call(f32[2,8,32,128]{3,2,1,0:T(8,128)S(1)} %bitcast.133, f32[2,8,32,128]{3,2,1,0:T(8,128)S(1)} %bitcast.128, f32[2,2,8,32,128]{4,3,2,1,0:T(8,128)S(1)} %convert_bitcast_fusion.perts, f32[2,5,16,8,128]{4,3,2,1,0:T(8,128)S(1)} %broadcast_in_dim.39.w_ref), custom_call_target="tpu_custom_call" | custom-call | tf_op jit(solution)/shard_map/backward/pallas_call | solution.py:311
  123.6 1.6 dynamic-slice_bitcast_fusion
  125.3 1.9 fusion.67
  127.2 1.3 maximum_bitcast_fusion
  128.6 1.5 copy.114
  131.1 4.7 %vertical.2 = (f32[2,8,32,128]{3,2,1,0:T(8,128)S(1)}, f32[2,8,32,128]{3,2,1,0:T(8,128)S(1)}) custom-call(f32[4,2,8,32,128]{4,3,2,1,0:T(8,128)S(1)} %get-tuple-element.22.full, f32[2,512,128]{2,1,0:T(8,128)S(1)} %bitcast.122, f32[2,8,32,128]{3,2,1,0:T(8,128)S(1)} %bitcast.135, f32[2,8,32,128]{3,2,1,0:T(8,128)S(1)} %bitcast.130), custom_call_target="tpu_custom_call" | custom-call | tf_op jit(solution)/shard_map/vertical/pallas_call | solution.py:311
  135.8 25.4 %forward.4 = f32[4,2,8,32,128]{4,3,2,1,0:T(8,128)S(1)} custom-call(f32[2,8,32,128]{3,2,1,0:T(8,128)S(1)} %get-tuple-element.24.mixed, f32[2,8,32,128]{3,2,1,0:T(8,128)S(1)} %copy-done.2, f32[2,2,8,32,128]{4,3,2,1,0:T(8,128)S(1)} %convert_bitcast_fusion.perts, f32[2,5,16,8,128]{4,3,2,1,0:T(8,128)S(1)} %broadcast_in_dim.39.w_ref), custom_call_target="tpu_custom_call" | custom-call | tf_op jit(solution)/shard_map/forward/pallas_call | solution.py:311
  162.1 2.4 %fusion.1 = f32[512,2048]{1,0:T(8,128)S(1)} fusion(s32[2048]{0:T(1024)S(1)} %bitcast.163, bf16[256,1024]{1,0:T(8,128)(2,1)S(1)} %get-tuple-element.46, bf16[256,1024]{1,0:T(8,128)(2,1)S(1)} %get-tuple-element.45), kind=kOutput, calls=%fused_computation.3 | convolution fusion | flops 2151677952 | bytes 5251072 | tf_op jit(solution)/shard_map/dot_general | solution.py:459
  168.4 1.9 fusion
  170.5 20.7 %backward.3 = (f32[4,2,8,32,128]{4,3,2,1,0:T(8,128)S(1)}, f32[2,8,32,128]{3,2,1,0:T(8,128)S(1)}) custom-call(f32[2,8,32,128]{3,2,1,0:T(8,128)S(1)} %bitcast.134, f32[2,8,32,128]{3,2,1,0:T(8,128)S(1)} %copy-done.2, f32[2,2,8,32,128]{4,3,2,1,0:T(8,128)S(1)} %convert_bitcast_fusion.perts, f32[2,5,16,8,128]{4,3,2,1,0:T(8,128)S(1)} %broadcast_in_dim.39.w_ref), custom_call_target="tpu_custom_call" | custom-call | tf_op jit(solution)/shard_map/backward/pallas_call | solution.py:311
  191.2 4.7 %vertical.3 = (f32[2,8,32,128]{3,2,1,0:T(8,128)S(1)}, f32[2,8,32,128]{3,2,1,0:T(8,128)S(1)}) custom-call(f32[4,2,8,32,128]{4,3,2,1,0:T(8,128)S(1)} %get-tuple-element.26.full, f32[2,512,128]{2,1,0:T(8,128)S(1)} %bitcast.123, f32[2,8,32,128]{3,2,1,0:T(8,128)S(1)} %get-tuple-element.27.static, f32[2,8,32,128]{3,2,1,0:T(8,128)S(1)} %get-tuple-element.24.mixed), custom_call_target="tpu_custom_call" | custom-call | tf_op jit(solution)/shard_map/vertical/pallas_call | solution.py:311
  196.0 17.8 %forward.5 = f32[2,8,32,128]{3,2,1,0:T(8,128)S(1)} custom-call(f32[2,8,32,128]{3,2,1,0:T(8,128)S(1)} %get-tuple-element.28.mixed, f32[2,8,32,128]{3,2,1,0:T(8,128)S(1)} %get-tuple-element.29.ensemble, f32[2,2,8,32,128]{4,3,2,1,0:T(8,128)S(1)} %convert_bitcast_fusion.perts, f32[2,5,16,8,128]{4,3,2,1,0:T(8,128)S(1)} %broadcast_in_dim.39.w_ref), custom_call_target="tpu_custom_call" | custom-call | tf_op jit(solution)/shard_map/forward/pallas_call | solution.py:311
  (105 shorter events, 21.0 us)
Async XLA Ops:
  7.2 6.9 %copy-start.12 = (f32[1,128,2,32]{1,3,2,0:T(8,128)S(1)}, f32[1,128,2,32]{1,3,2,0:T(8,128)}, u32[]{:S(2)}) copy-start(f32[1,128,2,32]{1,3,2,0:T(8,128)} %param.23) | copy-start | bytes 98308
  7.2 7.0 %copy-start.15 = (f32[8]{0:T(128)S(1)}, f32[8]{0:T(128)}, u32[]{:S(2)}) copy-start(f32[8]{0:T(128)} %param.19) | copy-start | bytes 100
  7.2 7.0 %copy-start.14 = (f32[8]{0:T(128)S(1)}, f32[8]{0:T(128)}, u32[]{:S(2)}) copy-start(f32[8]{0:T(128)} %param.20) | copy-start | bytes 100
  7.2 7.0 %copy-start.13 = (s32[8,128]{1,0:T(8,128)S(1)}, s32[8,128]{1,0:T(8,128)}, u32[]{:S(2)}) copy-start(s32[8,128]{1,0:T(8,128)} %param.18) | copy-start | bytes 12292
  7.2 7.1 %copy-start.3 = (f32[1,2,32,128]{3,2,1,0:T(8,128)S(1)}, f32[1,2,32,128]{3,2,1,0:T(8,128)}, u32[]{:S(2)}) copy-start(f32[1,2,32,128]{3,2,1,0:T(8,128)} %param.16) | copy-start | bytes 98308
  7.2 41.6 %all-gather.11.cloned.1.call-start = ((), (), s32[]{:S(2)}) async-start(), calls=%async_computation.3 | async-start | bytes 1310720 | tf_op jit(solution)/shard_map/all_gather | solution.py:453
  9.0 77.9 %all-gather.5.cloned.1.call-start = ((), (), s32[]{:S(2)}) async-start(), calls=%async_computation | async-start | bytes 2621440 | tf_op jit(solution)/shard_map/all_gather | solution.py:420
  14.4 31.7 %copy-start.16 = (s32[8]{0:T(128)S(1)}, s32[8]{0:T(128)}, u32[]{:S(2)}) copy-start(s32[8]{0:T(128)} %param.17) | copy-start | bytes 100
  44.2 3.5 %copy-start.9 = (f32[2,32,8,128]{3,2,1,0:T(8,128)S(1)}, f32[2,32,8,128]{3,2,1,0:T(8,128)}, u32[]{:S(2)}) copy-start(f32[2,32,8,128]{3,2,1,0:T(8,128)} %param.13) | copy-start | bytes 786436
  45.0 3.6 %copy-start.10 = (bf16[2,2,32,8,128]{4,3,2,1,0:T(8,128)(2,1)S(1)}, bf16[2,2,32,8,128]{4,3,2,1,0:T(8,128)(2,1)}, u32[]{:S(2)}) copy-start(bf16[2,2,32,8,128]{4,3,2,1,0:T(8,128)(2,1)} %param.15) | copy-start | bytes 786436
  45.1 52.5 %all-gather.7.cloned.1.call-start = ((), (), s32[]{:S(2)}) async-start(), calls=%async_computation.1 | async-start | bytes 1310720 | tf_op jit(solution)/shard_map/all_gather | solution.py:425
  45.1 3.6 %copy-start.11 = (f32[2,32,8,128]{3,2,1,0:T(8,128)S(1)}, f32[2,32,8,128]{3,2,1,0:T(8,128)}, u32[]{:S(2)}) copy-start(f32[2,32,8,128]{3,2,1,0:T(8,128)} %param.14) | copy-start | bytes 786436
  46.0 77.6 %all-gather.9.cloned.1.call-start = ((), (), s32[]{:S(2)}) async-start(), calls=%async_computation.2 | async-start | bytes 1310720 | tf_op jit(solution)/shard_map/all_gather | solution.py:428
  89.9 11.0 %copy-start.4 = (f32[1,8,4,32,256]{4,3,2,1,0:T(8,128)}, f32[1,8,4,32,256]{4,3,2,1,0:T(8,128)S(1)}, u32[]{:S(2)}) copy-start(f32[1,8,4,32,256]{4,3,2,1,0:T(8,128)S(1)} %copy.95) | copy-start | bytes 3145732
  122.9 0.7 copy-start.1
  123.6 1.7 copy-start.7
  130.1 1.0 copy-start
  131.1 4.7 %copy-start.2 = (f32[2,8,32,128]{3,2,1,0:T(8,128)S(1)}, f32[2,8,32,128]{3,2,1,0:T(8,128)}, u32[]{:S(2)}) copy-start(f32[2,8,32,128]{3,2,1,0:T(8,128)} %copy-done.1) | copy-start | bytes 786436
  164.5 1.2 copy-start.5
  164.5 1.5 copy-start.6
  164.5 1.8 copy-start.8
Sparse Core Ops, SparseCore 0:
  10.2 19.4 all-gather.10
  45.2 32.5 all-gather.4
  79.9 17.5 all-gather.6
  99.5 17.3 all-gather.8
